TPU v7x, 32 devices: a whole 2x2x4 slice. The times are simulated.
32 devices in a mesh: row: 8 (over y, x, core), col: 4 (over z).
Axes of the slice: x: 2, y: 2, z: 4, core: 2. Of those that a mesh axis runs over, the one named last changes fastest.
Arguments:
- latents: bfloat16 [512, 6144], P('col', 'row'), may hold values from -6 to 6
- w_in: bfloat16 [6144, 24576], P('row', 'col'), may hold values from -0.078125 to 0.078125
- w_out: bfloat16 [24576, 6144], P('col', 'row'), may hold values from -0.0390625 to 0.0390625
- cotangent: bfloat16 [512, 6144], P('col', 'row'), may hold values from -0.625 to 0.625
Outputs:
- mixed: bfloat16 [512, 6144], P('col', 'row')
- grad_w_in: bfloat16 [6144, 24576], P('row', 'col')
- grad_w_out: bfloat16 [24576, 6144], P('col', 'row')
All inputs are finite; a program needn't handle non-finite values.
Results may differ from a plain program's by a relative error of at most 0.03.
Values may be sent and summed in bfloat16 or wider, within the bound.
No kernel may reach another device: no remote copies, remote signals or barrier semaphores. Data moves between devices by JAX's collectives and lax.ppermute only.
A program may use at most 128 MiB of HBM per device.

v0:
```python
import jax
import jax.numpy as jnp
from jax import lax
from jax.sharding import PartitionSpec as P


def gelu_parts(hidden):
    cdf = 0.5 * (1.0 + jax.scipy.special.erf(hidden * 0.7071067811865476))
    pdf = jnp.exp(-0.5 * hidden * hidden) * 0.3989422804014327
    return (hidden * cdf, cdf + hidden * pdf)


def per_device(latents, w_in, w_out, cotangent):
    tokens_all = lax.all_gather(latents, "col", axis=0, tiled=True)
    block = tokens_all
    hidden = lax.psum_scatter(
        jnp.dot(block, w_in, preferred_element_type=jnp.float32).astype(jnp.bfloat16),
        "row",
        scatter_dimension=0,
        tiled=True,
    ).astype(jnp.float32)
    act, slope = gelu_parts(hidden)
    act = act.astype(jnp.bfloat16)
    act_all = lax.all_gather(act, "row", axis=0, tiled=True)
    block = act_all
    mixed = lax.psum_scatter(
        jnp.dot(block, w_out, preferred_element_type=jnp.float32).astype(jnp.bfloat16),
        "col",
        scatter_dimension=0,
        tiled=True,
    )
    cot_all = lax.all_gather(cotangent, "col", axis=0, tiled=True)
    block = cot_all
    grad_act = lax.psum_scatter(
        lax.dot_general(
            block, w_out, (((1,), (1,)), ((), ())), preferred_element_type=jnp.float32
        ).astype(jnp.bfloat16),
        "row",
        scatter_dimension=0,
        tiled=True,
    ).astype(jnp.float32)
    grad_hidden = (grad_act * slope).astype(jnp.bfloat16)
    grad_w_out = lax.dot_general(
        act_all, cot_all, (((0,), (0,)), ((), ())), preferred_element_type=jnp.float32
    )
    block = tokens_all
    grad_w_in = lax.dot_general(
        block,
        lax.all_gather(grad_hidden, "row", axis=0, tiled=True),
        (((0,), (0,)), ((), ())),
        preferred_element_type=jnp.float32,
    )
    return (mixed, grad_w_in.astype(jnp.bfloat16), grad_w_out.astype(jnp.bfloat16))


def solution(mesh):
    placed = (P("col", "row"), P("row", "col"), P("col", "row"), P("col", "row"))
    return jax.shard_map(
        per_device,
        mesh=mesh,
        in_specs=placed,
        out_specs=(P("col", "row"), P("row", "col"), P("col", "row")),
        check_vma=False,
    )
```

profile of v0, /device:TPU:0, one launch (start us, length us, event | category | flops | bytes accessed | tf_op | source)
XLA Modules:
  0.0 302.8 jit_solution(18334137243142497170)
XLA Ops:
  7.2 0.0 reduce-scatter.4.cloned.1.call-start
  7.2 21.5 %all_gather.12 = bf16[512,768]{1,0:T(8,128)(2,1)S(1)} all-gather(bf16[128,768]{1,0:T(8,128)(2,1)} %param.4), channel_id=1, replica_groups=mesh['row'=8,'col'=4] {'col'}, dimensions={0}, use_global_device_ids=true | all-gather | bytes 983040 | tf_op jit(solution)/shard_map/all_gather | solution.py:14
  28.7 10.6 %convolution_convert_fusion.3 = bf16[512,6144]{1,0:T(8,128)(2,1)} fusion(bf16[512,768]{1,0:T(8,128)(2,1)S(1)} %all_gather.12, bf16[768,6144]{1,0:T(8,128)(2,1)} %param.5), kind=kOutput, calls=%fused_computation.4 | convolution fusion | flops 4834983936 | bytes 16515072 | tf_op jit(solution)/shard_map/dot_general | solution.py:17
  39.3 0.0 reduce-scatter.4.cloned.1.call-update
  39.3 0.0 reduce-scatter.8.cloned.1.call-start
  39.4 0.9 copy-done
  40.2 17.7 %all_gather.14 = bf16[512,768]{1,0:T(8,128)(2,1)S(1)} all-gather(bf16[128,768]{1,0:T(8,128)(2,1)S(1)} %copy-done), channel_id=1, replica_groups=mesh['row'=8,'col'=4] {'col'}, dimensions={0}, use_global_device_ids=true | all-gather | bytes 983040 | tf_op jit(solution)/shard_map/all_gather | solution.py:32
  57.9 10.6 %convolution_convert_fusion.2 = bf16[512,6144]{1,0:T(8,128)(2,1)} fusion(bf16[512,768]{1,0:T(8,128)(2,1)S(1)} %all_gather.14, bf16[6144,768]{1,0:T(8,128)(2,1)} %param.6), kind=kOutput, calls=%fused_computation.3 | convolution fusion | flops 4834983936 | bytes 16515072 | tf_op jit(solution)/shard_map/dot_general | solution.py:35
  68.6 0.0 reduce-scatter.8.cloned.1.call-update
  68.6 0.0 all-gather.3.cloned.1.call-start
  68.6 31.9 %reduce-scatter.4.cloned.1.call-done = bf16[64,6144]{1,0:T(8,128)(2,1)} async-done(((bf16[512,6144]{1,0:T(8,128)(2,1)}), bf16[64,6144]{1,0:T(8,128)(2,1)}) %reduce-scatter.4.cloned.1.call-update) | async-done | bytes 786448 | tf_op jit(solution)/shard_map/reduce_scatter | solution.py:16
  100.6 66.1 %reduce-scatter.8.cloned.1.call-done = bf16[64,6144]{1,0:T(8,128)(2,1)} async-done(((bf16[512,6144]{1,0:T(8,128)(2,1)}), bf16[64,6144]{1,0:T(8,128)(2,1)}) %reduce-scatter.8.cloned.1.call-update) | async-done | bytes 786448 | tf_op jit(solution)/shard_map/reduce_scatter | solution.py:34
  166.7 3.3 %fusion.9 = (bf16[64,6144]{1,0:T(8,128)(2,1)}, bf16[64,6144]{1,0:T(8,128)(2,1)}) fusion(bf16[64,6144]{1,0:T(8,128)(2,1)} %reduce-scatter.4.cloned.1.call-done, bf16[64,6144]{1,0:T(8,128)(2,1)} %reduce-scatter.8.cloned.1.call-done), kind=kLoop, calls=%fused_computation.18 | loop fusion | flops 5505024 | bytes 3145728 | tf_op jit(solution)/shard_map/convert_element_type | solution.py:42
  170.0 0.0 all-gather.3.cloned.1.call-update
  170.0 0.0 all-gather.5.cloned.1.call-start
  170.1 0.5 all-gather.5.cloned.1.call-update
  170.6 0.2 reduce-scatter.6.cloned.1.call-start
  170.8 44.8 %all-gather.3.cloned.1.call-done = bf16[512,6144]{1,0:T(8,128)(2,1)} async-done(((bf16[64,6144]{1,0:T(8,128)(2,1)}), bf16[512,6144]{1,0:T(8,128)(2,1)}) %all-gather.3.cloned.1.call-update) | async-done | bytes 6291472 | tf_op jit(solution)/shard_map/all_gather | solution.py:24
  215.7 10.6 %convolution_convert_fusion.4 = bf16[512,768]{1,0:T(8,128)(2,1)} fusion(bf16[512,6144]{1,0:T(8,128)(2,1)} %all-gather.3.cloned.1.call-done, bf16[6144,768]{1,0:T(8,128)(2,1)} %param.6), kind=kOutput, calls=%fused_computation.19 | convolution fusion | flops 4832231424 | bytes 16515072 | tf_op jit(solution)/shard_map/dot_general | solution.py:27
  226.3 0.0 reduce-scatter.6.cloned.1.call-update
  226.3 37.2 %all-gather.5.cloned.1.call-done = bf16[512,6144]{1,0:T(8,128)(2,1)} async-done(((bf16[64,6144]{1,0:T(8,128)(2,1)}), bf16[512,6144]{1,0:T(8,128)(2,1)}) %all-gather.5.cloned.1.call-update) | async-done | bytes 6291472 | tf_op jit(solution)/shard_map/all_gather | solution.py:49
  263.5 10.1 %fusion = bf16[768,6144]{0,1:T(8,128)(2,1)} fusion(bf16[512,6144]{1,0:T(8,128)(2,1)} %all-gather.5.cloned.1.call-done, bf16[512,768]{1,0:T(8,128)(2,1)S(1)} %all_gather.12), kind=kOutput, calls=%fused_computation.2 | convolution fusion | flops 4836556800 | bytes 16515072 | tf_op jit(solution)/shard_map/dot_general | solution.py:47
  273.6 12.6 %copy.7 = bf16[768,6144]{1,0:T(8,128)(2,1)} copy(bf16[768,6144]{0,1:T(8,128)(2,1)} %fusion) | data formatting | bytes 18874368
  286.2 10.1 %convolution_convert_fusion = bf16[6144,768]{1,0:T(8,128)(2,1)} fusion(bf16[512,6144]{1,0:T(8,128)(2,1)} %all-gather.3.cloned.1.call-done, bf16[512,768]{1,0:T(8,128)(2,1)S(1)} %all_gather.14), kind=kOutput, calls=%fused_computation | convolution fusion | flops 4836556800 | bytes 16515072 | tf_op jit(solution)/shard_map/dot_general | solution.py:43
  (2 shorter events, 0.0 us)
Async XLA Ops:
  7.2 93.4 %reduce-scatter.4.cloned.1.call-start = ((), (), s32[]{:S(2)}) async-start(), calls=%async_computation.3 | async-start | bytes 7077888 | tf_op jit(solution)/shard_map/reduce_scatter | solution.py:16
  39.3 0.9 copy-start
  39.3 127.3 %reduce-scatter.8.cloned.1.call-start = ((), (), s32[]{:S(2)}) async-start(), calls=%async_computation.6 | async-start | bytes 7077888 | tf_op jit(solution)/shard_map/reduce_scatter | solution.py:34
  68.6 147.1 %all-gather.3.cloned.1.call-start = ((), (), s32[]{:S(2)}) async-start(), calls=%async_computation.4 | async-start | bytes 7077888 | tf_op jit(solution)/shard_map/all_gather | solution.py:24
  170.0 93.5 %all-gather.5.cloned.1.call-start = ((), (), s32[]{:S(2)}) async-start(), calls=%async_computation.7 | async-start | bytes 7077888 | tf_op jit(solution)/shard_map/all_gather | solution.py:49
  170.6 125.7 %reduce-scatter.6.cloned.1.call-start = ((), (), s32[]{:S(2)}) async-start(), calls=%async_computation.5 | async-start | bytes 983040 | tf_op jit(solution)/shard_map/reduce_scatter | solution.py:26
Sparse Core Ops, SparseCore 0:
  39.4 61.0 reduce-scatter.3
  104.9 61.7 reduce-scatter.7
  170.1 45.4 all-gather.2
  218.0 45.5 all-gather.4
  266.3 23.2 reduce-scatter.5
where the time goes:
time: 303 us
  waiting for transfers between devices  181 us (60%)
  matrix products  52 us (17%)
  blocking collectives  39.2 us (13%)
  between operations  13.8 us (5%)
  local copies, waits for them, and re-layouts  13.5 us (4%)
  other arithmetic  3.32 us (1%)
    reduce_scatter x1, waiting for transfers between devices, per_device(): lax.psum_scatter(lax.dot_general(block, w_out, (((1,), (1,)), ((), ())),...  66.1 us
    all_gather x1, waiting for transfers between devices, per_device(): act_all = lax.all_gather(act, 'row', axis=0, tiled=True)  44.8 us
    all_gather x1, waiting for transfers between devices, per_device(): lax.all_gather(grad_hidden, 'row', axis=0, tiled=True)  37.2 us
    reduce_scatter x1, waiting for transfers between devices, per_device(): lax.psum_scatter(jnp.dot(block, w_in, preferred_element_type=jnp.float32)...  31.9 us
    all_gather x1, blocking collectives, per_device(): tokens_all = lax.all_gather(latents, 'col', axis=0, tiled=True)  21.5 us
    all_gather x1, blocking collectives, per_device(): cot_all = lax.all_gather(cotangent, 'col', axis=0, tiled=True)  17.7 us
    unnamed x3, local copies, waits for them, and re-layouts  13.5 us
    dot_general x1, matrix products, per_device(): lax.dot_general(block, w_out, (((1,), (1,)), ((), ())), preferred_element...  10.6 us
  transfers between devices with their start and end apart: 5, of which 4 were waited for; matrix products, arithmetic and copies ran while one was open for 18% of the time, Pallas kernels for 0%

commit v1 on v0

v1 whole, which is shorter than its diff:
```python
import jax
import jax.numpy as jnp
from jax import lax
from jax.sharding import PartitionSpec as P

f32 = jnp.float32
bf16 = jnp.bfloat16


def gelu_parts(hidden):
    cdf = 0.5 * (1.0 + jax.scipy.special.erf(hidden * 0.7071067811865476))
    pdf = jnp.exp(-0.5 * hidden * hidden) * 0.3989422804014327
    return (hidden * cdf, cdf + hidden * pdf)


def make(n_row, n_col):
    row_bits = n_row.bit_length() - 1
    col_bits = n_col.bit_length() - 1
    first = tuple(range(1, row_bits))
    orders = (first, first[::-1])
    steps = len(first)

    def swap_core(v):
        return lax.ppermute(v, "row", [(i, i ^ 1) for i in range(n_row)])

    def swap_chip(v, step):
        return lax.ppermute(v, "row", [(i, i ^ (1 << orders[i & 1][step])) for i in range(n_row)])

    def swap_col(v, bit):
        return lax.ppermute(v, "col", [(i, i ^ (1 << bit)) for i in range(n_col)])

    def part(v, axis, index):
        return lax.slice_in_dim(v, index, index + 1, axis=axis)

    def flips(v, order, axis):
        me = lax.axis_index("row")
        for k, bit in enumerate(order):
            v = jnp.where((me >> bit) & 1 == 1, jnp.flip(v, axis + k), v)
        return v

    def relative(v):
        v = v.reshape((2,) * steps + (1, v.shape[0] >> steps, v.shape[1]))
        return flips(v, first, 0)

    def turn(v):
        return v.transpose(tuple(range(steps))[::-1] + tuple(range(steps, v.ndim)))

    def after(v, *tokens):
        return lax.optimization_barrier((v,) + tokens)[0]

    def flat(v):
        return v.reshape(-1, v.shape[-1])

    def scatter(parts):
        core = lax.axis_index("row") & 1
        second = turn(parts[1])
        got = swap_core(jnp.where(core == 0, second, parts[0]))
        v = jnp.where(core == 0, parts[0], second)
        v = (v.astype(f32) + got.astype(f32)).astype(bf16)
        seen = [v]
        for k in range(steps):
            got = swap_chip(part(v, k, 1), k)
            seen.append(got)
            v = part(v, k, 0).astype(f32) + got.astype(f32)
            if k + 1 < steps:
                v = v.astype(bf16)
        return v, seen

    def gather_chips(v, stop):
        for k in reversed(range(stop, steps)):
            v = lax.concatenate([v, swap_chip(v, k)], k)
        return v

    def per_device(latents, w_in, w_out, cotangent):
        tokens, width = latents.shape
        cut = w_in.shape[1] // 2
        core = lax.axis_index("row") & 1

        def double(v, bit):
            got = swap_col(v, bit)
            return got, lax.concatenate([v, got], steps)

        halves = [slice(h * cut, (h + 1) * cut) for h in (0, 1)]

        def up(x):
            parts = [jnp.dot(flat(x), w_in[:, h], preferred_element_type=f32) for h in halves]
            return scatter([v.astype(bf16).reshape(x.shape[:-1] + (cut,)) for v in parts])

        def back(c):
            parts = [
                lax.dot_general(flat(c), w_out[h], (((1,), (1,)), ((), ())), preferred_element_type=f32)
                for h in halves
            ]
            return scatter([v.astype(bf16).reshape(c.shape[:-1] + (cut,)) for v in parts])

        _, x_all = double(relative(latents), 0)
        _, c_all = double(relative(cotangent), 0)
        hid, seen_hid = up(x_all)
        grad, seen_grad = back(c_all)
        hids, grads = [hid], [grad]
        for bit in range(1, col_bits):
            x, x_all = double(x_all, bit)
            x = after(x, seen_hid[1], seen_grad[0])
            c, c_all = double(after(c_all, x), bit)
            hid, seen_hid = up(x)
            grad, seen_grad = back(after(c, seen_grad[1], seen_hid[1]))
            hids.append(hid)
            grads.append(grad)

        hid = jnp.concatenate(hids, steps)
        act = gelu_parts(hid)[0].astype(bf16)
        grad = jnp.concatenate(grads, steps)
        hid, grad = lax.optimization_barrier((hid, grad))
        grad = (grad * gelu_parts(hid)[1]).astype(bf16)

        def gather(v):
            v = gather_chips(v, 1)
            quarter = cut // 2
            firsts, seconds = [], []
            for p in range(2):
                w = gather_chips_last(v[..., p * quarter : (p + 1) * quarter])
                got = swap_core(w)
                firsts.append(jnp.where(core == 0, w, got))
                seconds.append(turn(jnp.where(core == 0, got, w)))
            return lax.optimization_barrier(lax.concatenate(firsts + seconds, steps + 2))

        def gather_chips_last(v):
            return lax.concatenate([v, swap_chip(v, 0)], 0)

        act_all = gather(act)
        grad_all = gather(grad)
        lead = act_all.shape[:-1]

        mixed = jnp.dot(flat(act_all), w_out, preferred_element_type=f32).astype(bf16).reshape(lead + (width,))
        for bit in reversed(range(col_bits)):
            blocks = mixed.shape[steps] // 2
            got = swap_col(lax.slice_in_dim(mixed, blocks, 2 * blocks, axis=steps), bit)
            keep = lax.slice_in_dim(mixed, 0, blocks, axis=steps)
            mixed = (keep.astype(f32) + got.astype(f32)).astype(bf16)
        mixed = flips(mixed, first, 0).reshape(tokens, width)

        grad_w_out = lax.dot_general(
            flat(act_all), flat(c_all), (((0,), (0,)), ((), ())), preferred_element_type=f32
        )
        x_t = lax.optimization_barrier(flat(x_all).T)
        grad_w_in = jnp.dot(x_t, flat(grad_all), preferred_element_type=f32)
        return (mixed, grad_w_in.astype(bf16), grad_w_out.astype(bf16))

    return per_device


def solution(mesh):
    placed = (P("col", "row"), P("row", "col"), P("col", "row"), P("col", "row"))
    return jax.shard_map(
        make(mesh.shape["row"], mesh.shape["col"]),
        mesh=mesh,
        in_specs=placed,
        out_specs=(P("col", "row"), P("row", "col"), P("col", "row")),
        check_vma=False,
    )
```

time: 303 us -> 193 us (0.64)
  waiting for transfers between devices: 181 us -> 104 us
  blocking collectives: 39.2 us -> 0 us
  starting transfers between devices: 0.38 us -> 27.2 us
  other arithmetic: 3.32 us -> 22.2 us
  matrix products: 52 us -> 34.4 us
  between operations: 13.8 us -> 1.18 us
  local copies, waits for them, and re-layouts: 13.5 us -> 3.48 us
    ppermute x0 -> x28, waiting for transfers between devices: none -> 104 us  [the longest x14 55.7 us: swap_chip(): lax.ppermute(v, 'row', [(i, i ^ 1 << orders[i & 1][step]) for i in range(...]
    reduce_scatter x3 -> x0, waiting for transfers between devices: 98 us -> none  [the longest x1 66.1 us: per_device(): lax.psum_scatter(lax.dot_general(block, w_out, (((1,), (1,)), ((), ())),...]
    all_gather x2 -> x0, waiting for transfers between devices: 82.1 us -> none  [the longest x1 44.8 us: per_device(): act_all = lax.all_gather(act, 'row', axis=0, tiled=True)]
    all_gather x2 -> x0, blocking collectives: 39.2 us -> none  [the longest x1 21.5 us: per_device(): tokens_all = lax.all_gather(latents, 'col', axis=0, tiled=True)]
    ppermute x0 -> x28, starting transfers between devices: none -> 27.2 us  [the longest x14 19.7 us: swap_chip(): lax.ppermute(v, 'row', [(i, i ^ 1 << orders[i & 1][step]) for i in range(...]
    dot_general x5 -> x11, matrix products: 52 us -> 34.4 us  [the longest x4 8.15 us: up(): jnp.dot(flat(x), w_in[:, h], preferred_element_type=f32)]
    concatenate x0 -> x13, other arithmetic: none -> 12.7 us  [the longest x2 11.1 us: gather(): lax.concatenate(firsts + seconds, steps + 2)]
    unnamed x3 -> x4, local copies, waits for them, and re-layouts: 13.5 us -> 3.12 us
  transfers between devices with their start and end apart: 5 -> 28, of which waited for: 4 -> 13; matrix products, arithmetic and copies ran while one was open for 18% -> 20% of each run, Pallas kernels for 0% -> 0%
where the time goes in v1:
time: 193 us
  waiting for transfers between devices  104 us (54%)
  matrix products  34.4 us (18%)
  starting transfers between devices  27.2 us (14%)
  other arithmetic  22.2 us (12%)
  local copies, waits for them, and re-layouts  3.48 us (2%)
    ppermute x14, waiting for transfers between devices, swap_chip(): lax.ppermute(v, 'row', [(i, i ^ 1 << orders[i & 1][step]) for i in range(...  55.7 us
    ppermute x6, waiting for transfers between devices, swap_col(): return lax.ppermute(v, 'col', [(i, i ^ 1 << bit) for i in range(n_col)])  46.1 us
    ppermute x14, starting transfers between devices, swap_chip(): lax.ppermute(v, 'row', [(i, i ^ 1 << orders[i & 1][step]) for i in range(...  19.7 us
    concatenate x2, other arithmetic, gather(): lax.concatenate(firsts + seconds, steps + 2)  11.1 us
    dot_general x4, matrix products, up(): jnp.dot(flat(x), w_in[:, h], preferred_element_type=f32)  8.15 us
    dot_general x1, matrix products, per_device(): lax.dot_general(flat(act_all), flat(c_all), (((0,), (0,)), ((), ())), pre...  7.64 us
    dot_general x1, matrix products, per_device(): grad_w_in = jnp.dot(x_t, flat(grad_all), preferred_element_type=f32)  7.58 us
    ppermute x6, starting transfers between devices, swap_col(): return lax.ppermute(v, 'col', [(i, i ^ 1 << bit) for i in range(n_col)])  6.45 us
  transfers between devices with their start and end apart: 28, of which 13 were waited for; matrix products, arithmetic and copies ran while one was open for 20% of the time, Pallas kernels for 0%

profile of v1, /device:TPU:0, one launch (start us, length us, event | category | flops | bytes accessed | tf_op | source)
XLA Modules:
  0.0 192.6 jit_solution(6193675513724014893)
XLA Ops:
  1.8 3.1 %collective-permute-start = (bf16[2,2,1,32,768]{4,3,2,1,0:T(8,128)(2,1)S(1)}, bf16[2,2,1,32,768]{4,3,2,1,0:T(8,128)(2,1)S(1)}, u32[]{:S(2)}, u32[]{:S(2)}) collective-permute-start(bf16[2,2,1,32,768]{4,3,2,1,0:T(8,128)(2,1)S(1)} %reverse_select_fusion.4), channel_id=1, source_target_pairs={{0,1},{1,0},{2,3},{3,2},{4,5},{5,4},{6,7},{7,6},{8,9},{9,8},{10,11... | collective-permute-start | bytes 589832 | tf_op jit(solution)/shard_map/ppermute | solution.py:30
  6.0 4.5 %collective-permute-done = bf16[2,2,1,32,768]{4,3,2,1,0:T(8,128)(2,1)S(1)} collective-permute-done((bf16[2,2,1,32,768]{4,3,2,1,0:T(8,128)(2,1)S(1)}, bf16[2,2,1,32,768]{4,3,2,1,0:T(8,128)(2,1)S(1)}, u32[]{:S(2)}, u32[]{:S(2)}) %collective-permute-start) | collective-permute-done | bytes 196640 | tf_op jit(solution)/shard_map/ppermute | solution.py:30
  10.6 3.9 %fusion.16 = bf16[256,3072]{1,0:T(8,128)(2,1)S(1)} fusion(bf16[256,768]{1,0:T(8,128)(2,1)S(1)} %bitcast.77, bf16[768,6144]{1,0:T(8,128)(2,1)} %param.5), kind=kOutput, calls=%fused_computation.20 | convolution fusion | flops 1208745984 | bytes 6684672 | tf_op jit(solution)/shard_map/dot_general | solution.py:86
  17.4 2.0 %copy-done.1 = bf16[6144,768]{1,0:T(8,128)(2,1)S(1)} copy-done((bf16[6144,768]{1,0:T(8,128)(2,1)S(1)}, bf16[6144,768]{1,0:T(8,128)(2,1)}, u32[]{:S(2)}) %copy-start.1) | copy-done | bytes 9437208
  22.5 3.1 %collective-permute-start.4 = (bf16[2,2,2,32,768]{4,3,2,1,0:T(8,128)(2,1)S(1)}, bf16[2,2,2,32,768]{4,3,2,1,0:T(8,128)(2,1)S(1)}, u32[]{:S(2)}, u32[]{:S(2)}) collective-permute-start(bf16[2,2,2,32,768]{4,3,2,1,0:T(8,128)(2,1)S(1)} %pad_maximum_fusion.11), channel_id=1, source_target_pairs={{0,2},{1,3},{2,0},{3,1},{4,6},{5,7},{6,4},{7,5},{8,10},{9,11},{10,... | collective-permute-start | bytes 1179656 | tf_op jit(solution)/shard_map/ppermute | solution.py:30
  28.9 14.9 %collective-permute-done.4 = bf16[2,2,2,32,768]{4,3,2,1,0:T(8,128)(2,1)S(1)} collective-permute-done((bf16[2,2,2,32,768]{4,3,2,1,0:T(8,128)(2,1)S(1)}, bf16[2,2,2,32,768]{4,3,2,1,0:T(8,128)(2,1)S(1)}, u32[]{:S(2)}, u32[]{:S(2)}) %collective-permute-start.4) | collective-permute-done | bytes 393248 | tf_op jit(solution)/shard_map/ppermute | solution.py:30
  48.6 1.7 collective-permute-done.7
  52.8 6.2 %collective-permute-done.17 = bf16[1,2,2,32,3072]{4,3,2,0,1:T(8,128)(2,1)S(1)} collective-permute-done((bf16[1,2,2,32,3072]{4,3,2,0,1:T(8,128)(2,1)S(1)}, bf16[1,2,2,32,3072]{4,3,2,0,1:T(8,128)(2,1)S(1)}, u32[]{:S(2)}, u32[]{:S(2)}) %collective-permute-start.17) | collective-permute-done | bytes 786464 | tf_op jit(solution)/shard_map/ppermute | solution.py:27
  61.7 7.5 %collective-permute-done.19 = bf16[2,2,2,32,768]{4,3,2,1,0:T(8,128)(2,1)S(1)} collective-permute-done((bf16[2,2,2,32,768]{4,3,2,1,0:T(8,128)(2,1)S(1)}, bf16[2,2,2,32,768]{4,3,2,1,0:T(8,128)(2,1)S(1)}, u32[]{:S(2)}, u32[]{:S(2)}) %collective-permute-start.19) | collective-permute-done | bytes 393248 | tf_op jit(solution)/shard_map/ppermute | solution.py:30
  69.2 4.1 %collective-permute-done.8 = bf16[1,2,2,32,3072]{4,3,2,0,1:T(8,128)(2,1)S(1)} collective-permute-done((bf16[1,2,2,32,3072]{4,3,2,0,1:T(8,128)(2,1)S(1)}, bf16[1,2,2,32,3072]{4,3,2,0,1:T(8,128)(2,1)S(1)}, u32[]{:S(2)}, u32[]{:S(2)}) %collective-permute-start.8) | collective-permute-done | bytes 786464 | tf_op jit(solution)/shard_map/ppermute | solution.py:27
  76.8 1.6 collective-permute-start.9
  78.6 6.1 %collective-permute-done.9 = bf16[1,1,2,32,3072]{4,3,2,0,1:T(8,128)(2,1)S(1)} collective-permute-done((bf16[1,1,2,32,3072]{4,3,2,0,1:T(8,128)(2,1)S(1)}, bf16[1,1,2,32,3072]{4,3,2,0,1:T(8,128)(2,1)S(1)}, u32[]{:S(2)}, u32[]{:S(2)}) %collective-permute-start.9) | collective-permute-done | bytes 393248 | tf_op jit(solution)/shard_map/ppermute | solution.py:27
  89.2 15.6 %collective-permute-done.10 = bf16[1,1,4,32,3072]{4,3,2,0,1:T(8,128)(2,1)S(1)} collective-permute-done((bf16[1,1,4,32,3072]{4,3,2,0,1:T(8,128)(2,1)S(1)}, bf16[1,1,4,32,3072]{4,3,2,0,1:T(8,128)(2,1)S(1)}, u32[]{:S(2)}, u32[]{:S(2)}) %collective-permute-start.10) | collective-permute-done | bytes 786464 | tf_op jit(solution)/shard_map/ppermute | solution.py:27
  104.9 2.5 %collective-permute-start.11 = (bf16[1,2,4,32,1536]{4,3,2,0,1:T(8,128)(2,1)S(1)}, bf16[1,2,4,32,1536]{4,3,2,0,1:T(8,128)(2,1)S(1)}, u32[]{:S(2)}, u32[]{:S(2)}) collective-permute-start(bf16[1,2,4,32,1536]{4,3,2,0,1:T(8,128)(2,1)S(1)} %get-tuple-element.25), channel_id=1, source_target_pairs={{0,8},{4,20},{8,0},{12,28},{16,24},{20,4},{24,16},{28,12},{1,9},{5... | collective-permute-start | bytes 2359304 | tf_op jit(solution)/shard_map/ppermute | solution.py:27
  109.4 11.6 %collective-permute-done.11 = bf16[1,2,4,32,1536]{4,3,2,0,1:T(8,128)(2,1)S(1)} collective-permute-done((bf16[1,2,4,32,1536]{4,3,2,0,1:T(8,128)(2,1)S(1)}, bf16[1,2,4,32,1536]{4,3,2,0,1:T(8,128)(2,1)S(1)}, u32[]{:S(2)}, u32[]{:S(2)}) %collective-permute-start.11) | collective-permute-done | bytes 786464 | tf_op jit(solution)/shard_map/ppermute | solution.py:27
  121.2 8.2 %collective-permute-done.13 = bf16[1,2,4,32,1536]{4,3,2,0,1:T(8,128)(2,1)S(1)} collective-permute-done((bf16[1,2,4,32,1536]{4,3,2,0,1:T(8,128)(2,1)S(1)}, bf16[1,2,4,32,1536]{4,3,2,0,1:T(8,128)(2,1)S(1)}, u32[]{:S(2)}, u32[]{:S(2)}) %collective-permute-start.13) | collective-permute-done | bytes 786464 | tf_op jit(solution)/shard_map/ppermute | solution.py:27
  130.5 1.6 collective-permute-start.23
  133.2 5.5 %pad_maximum_fusion = bf16[2,2,4,32,6144]{4,3,2,1,0:T(8,128)(2,1)S(1)} fusion(bf16[2,2,4,32,1536]{4,3,2,1,0:T(8,128)(2,1)S(1)} %get-tuple-element.20, bf16[2,2,4,32,1536]{4,3,2,1,0:T(8,128)(2,1)S(1)} %get-tuple-element.18, bf16[2,2,4,32,1536]{4,3,2,0,1:T(8,128)(2,1)S(1)} %get-tuple-element.17, bf16[2,2,4,32,1536]{4,3,2,0,1:T(8,128)(2,1)S(1)} %get-tuple-element.19), kind=kLoop, calls=%fused_computation.2 | loop fusion | flops 25165824 | bytes 12582912 | tf_op jit(solution)/shard_map/concatenate | solution.py:125
  138.7 3.8 %collective-permute-done.23 = bf16[1,1,4,32,3072]{4,3,2,0,1:T(8,128)(2,1)S(1)} collective-permute-done((bf16[1,1,4,32,3072]{4,3,2,0,1:T(8,128)(2,1)S(1)}, bf16[1,1,4,32,3072]{4,3,2,0,1:T(8,128)(2,1)S(1)}, u32[]{:S(2)}, u32[]{:S(2)}) %collective-permute-start.23) | collective-permute-done | bytes 786464 | tf_op jit(solution)/shard_map/ppermute | solution.py:27
  144.2 5.1 %convolution_convert_fusion.1 = bf16[512,768]{1,0:T(8,128)(2,1)S(1)} fusion(bf16[512,6144]{1,0:T(8,128)(2,1)S(1)} %bitcast.54, bf16[6144,768]{1,0:T(8,128)(2,1)S(1)} %copy-done.1), kind=kOutput, calls=%fused_computation.66 | convolution fusion | flops 4832231424 | bytes 16515072 | tf_op jit(solution)/shard_map/dot_general | solution.py:134
  150.2 19.1 %collective-permute-done.15 = bf16[2,2,2,32,768]{4,3,2,1,0:T(8,128)(2,1)S(1)} collective-permute-done((bf16[2,2,2,32,768]{4,3,2,1,0:T(8,128)(2,1)S(1)}, bf16[2,2,2,32,768]{4,3,2,1,0:T(8,128)(2,1)S(1)}, u32[]{:S(2)}, u32[]{:S(2)}) %collective-permute-start.15) | collective-permute-done | bytes 393248 | tf_op jit(solution)/shard_map/ppermute | solution.py:30
  170.4 7.6 %bitcast_convert_fusion = bf16[6144,768]{1,0:T(8,128)(2,1)} fusion(bf16[2,2,4,32,6144]{4,3,2,1,0:T(8,128)(2,1)S(1)} %pad_maximum_fusion, bf16[2,2,2,32,768]{4,3,2,1,0:T(8,128)(2,1)S(1)} %collective-permute-done.19, bf16[2,2,2,32,768]{4,3,2,1,0:T(8,128)(2,1)S(1)} %pad_maximum_fusion.12), kind=kOutput, calls=%fused_computation | convolution fusion | flops 4836950016 | bytes 16515072 | tf_op jit(solution)/shard_map/dot_general | solution.py:142
  179.3 5.7 %pad_maximum_fusion.1 = bf16[2,2,4,32,6144]{4,3,2,1,0:T(8,128)(2,1)S(1)} fusion(bf16[2,2,4,32,1536]{4,3,2,1,0:T(8,128)(2,1)S(1)} %get-tuple-element.16, bf16[2,2,4,32,1536]{4,3,2,1,0:T(8,128)(2,1)S(1)} %get-tuple-element.14, bf16[2,2,4,32,1536]{4,3,2,0,1:T(8,128)(2,1)S(1)} %get-tuple-element.13, bf16[2,2,4,32,1536]{4,3,2,0,1:T(8,128)(2,1)S(1)} %get-tuple-element.15), kind=kLoop, calls=%fused_computation.3 | loop fusion | flops 25165824 | bytes 12582912 | tf_op jit(solution)/shard_map/concatenate | solution.py:125
  185.0 7.6 %convolution_convert_fusion = bf16[768,6144]{1,0:T(8,128)(2,1)} fusion(bf16[768,512]{0,1:T(8,128)(2,1)S(1)} %bitcast.72, bf16[512,6144]{1,0:T(8,128)(2,1)S(1)} %bitcast.55), kind=kOutput, calls=%fused_computation.1 | convolution fusion | flops 4836556800 | bytes 16515072 | tf_op jit(solution)/shard_map/dot_general | solution.py:146
  (99 shorter events, 38.7 us)
Async XLA Ops:
  1.8 8.8 %collective-permute-start = (bf16[2,2,1,32,768]{4,3,2,1,0:T(8,128)(2,1)S(1)}, bf16[2,2,1,32,768]{4,3,2,1,0:T(8,128)(2,1)S(1)}, u32[]{:S(2)}, u32[]{:S(2)}) collective-permute-start(bf16[2,2,1,32,768]{4,3,2,1,0:T(8,128)(2,1)S(1)} %reverse_select_fusion.4), channel_id=1, source_target_pairs={{0,1},{1,0},{2,3},{3,2},{4,5},{5,4},{6,7},{7,6},{8,9},{9,8},{10,11... | collective-permute-start | bytes 589832 | tf_op jit(solution)/shard_map/ppermute | solution.py:30
  6.0 11.4 %collective-permute-start.5 = (bf16[2,2,1,32,768]{4,3,2,1,0:T(8,128)(2,1)S(1)}, bf16[2,2,1,32,768]{4,3,2,1,0:T(8,128)(2,1)S(1)}, u32[]{:S(2)}, u32[]{:S(2)}) collective-permute-start(bf16[2,2,1,32,768]{4,3,2,1,0:T(8,128)(2,1)S(1)} %reverse_select_fusion.2), channel_id=1, source_target_pairs={{0,1},{1,0},{2,3},{3,2},{4,5},{5,4},{6,7},{7,6},{8,9},{9,8},{10,11... | collective-permute-start | bytes 589832 | tf_op jit(solution)/shard_map/ppermute | solution.py:30
  17.2 8.4 %collective-permute-start.1 = (bf16[2,2,2,32,3072]{4,3,2,0,1:T(8,128)(2,1)S(1)}, bf16[2,2,2,32,3072]{4,3,2,0,1:T(8,128)(2,1)S(1)}, u32[]{:S(2)}, u32[]{:S(2)}) collective-permute-start(bf16[2,2,2,32,3072]{4,3,2,0,1:T(8,128)(2,1)S(1)} %broadcast_select_fusion.3), channel_id=1, source_target_pairs={{0,4},{4,0},{8,12},{12,8},{16,20},{20,16},{24,28},{28,24},{1,5},{5... | collective-permute-start | bytes 4718600 | tf_op jit(solution)/shard_map/ppermute | solution.py:24
  22.5 21.3 %collective-permute-start.4 = (bf16[2,2,2,32,768]{4,3,2,1,0:T(8,128)(2,1)S(1)}, bf16[2,2,2,32,768]{4,3,2,1,0:T(8,128)(2,1)S(1)}, u32[]{:S(2)}, u32[]{:S(2)}) collective-permute-start(bf16[2,2,2,32,768]{4,3,2,1,0:T(8,128)(2,1)S(1)} %pad_maximum_fusion.11), channel_id=1, source_target_pairs={{0,2},{1,3},{2,0},{3,1},{4,6},{5,7},{6,4},{7,5},{8,10},{9,11},{10,... | collective-permute-start | bytes 1179656 | tf_op jit(solution)/shard_map/ppermute | solution.py:30
  26.5 17.3 %collective-permute-start.2 = (bf16[1,2,2,32,3072]{4,3,2,0,1:T(8,128)(2,1)S(1)}, bf16[1,2,2,32,3072]{4,3,2,0,1:T(8,128)(2,1)S(1)}, u32[]{:S(2)}, u32[]{:S(2)}) collective-permute-start(bf16[1,2,2,32,3072]{4,3,2,0,1:T(8,128)(2,1)S(1)} %slice.117), channel_id=1, source_target_pairs={{0,8},{4,20},{8,0},{12,28},{16,24},{20,4},{24,16},{28,12},{1,9},{5... | collective-permute-start | bytes 2359304 | tf_op jit(solution)/shard_map/ppermute | solution.py:27
  47.0 12.1 %collective-permute-start.17 = (bf16[1,2,2,32,3072]{4,3,2,0,1:T(8,128)(2,1)S(1)}, bf16[1,2,2,32,3072]{4,3,2,0,1:T(8,128)(2,1)S(1)}, u32[]{:S(2)}, u32[]{:S(2)}) collective-permute-start(bf16[1,2,2,32,3072]{4,3,2,0,1:T(8,128)(2,1)S(1)} %slice.131), channel_id=1, source_target_pairs={{0,8},{4,20},{8,0},{12,28},{16,24},{20,4},{24,16},{28,12},{1,9},{5... | collective-permute-start | bytes 2359304 | tf_op jit(solution)/shard_map/ppermute | solution.py:27
  48.6 20.6 %collective-permute-start.19 = (bf16[2,2,2,32,768]{4,3,2,1,0:T(8,128)(2,1)S(1)}, bf16[2,2,2,32,768]{4,3,2,1,0:T(8,128)(2,1)S(1)}, u32[]{:S(2)}, u32[]{:S(2)}) collective-permute-start(bf16[2,2,2,32,768]{4,3,2,1,0:T(8,128)(2,1)S(1)} %pad_maximum_fusion.12), channel_id=1, source_target_pairs={{0,2},{1,3},{2,0},{3,1},{4,6},{5,7},{6,4},{7,5},{8,10},{9,11},{10,... | collective-permute-start | bytes 1179656 | tf_op jit(solution)/shard_map/ppermute | solution.py:30
  51.2 22.1 %collective-permute-start.8 = (bf16[1,2,2,32,3072]{4,3,2,0,1:T(8,128)(2,1)S(1)}, bf16[1,2,2,32,3072]{4,3,2,0,1:T(8,128)(2,1)S(1)}, u32[]{:S(2)}, u32[]{:S(2)}) collective-permute-start(bf16[1,2,2,32,3072]{4,3,2,0,1:T(8,128)(2,1)S(1)} %slice.121), channel_id=1, source_target_pairs={{0,8},{4,20},{8,0},{12,28},{16,24},{20,4},{24,16},{28,12},{1,9},{5... | collective-permute-start | bytes 2359304 | tf_op jit(solution)/shard_map/ppermute | solution.py:27
  59.3 48.1 %collective-permute-start.18 = (bf16[1,1,2,32,3072]{4,3,2,0,1:T(8,128)(2,1)S(1)}, bf16[1,1,2,32,3072]{4,3,2,0,1:T(8,128)(2,1)S(1)}, u32[]{:S(2)}, u32[]{:S(2)}) collective-permute-start(bf16[1,1,2,32,3072]{4,3,2,0,1:T(8,128)(2,1)S(1)} %slice.133), channel_id=1, source_target_pairs={{0,16},{4,12},{8,24},{12,4},{16,0},{20,28},{24,8},{28,20},{1,17},{... | collective-permute-start | bytes 1179656 | tf_op jit(solution)/shard_map/ppermute | solution.py:27
  61.2 17.3 %collective-permute-start.3 = (bf16[1,1,2,32,3072]{4,3,2,0,1:T(8,128)(2,1)S(1)}, bf16[1,1,2,32,3072]{4,3,2,0,1:T(8,128)(2,1)S(1)}, u32[]{:S(2)}, u32[]{:S(2)}) collective-permute-start(bf16[1,1,2,32,3072]{4,3,2,0,1:T(8,128)(2,1)S(1)} %slice.119), channel_id=1, source_target_pairs={{0,16},{4,12},{8,24},{12,4},{16,0},{20,28},{24,8},{28,20},{1,17},{... | collective-permute-start | bytes 1179656 | tf_op jit(solution)/shard_map/ppermute | solution.py:27
  76.5 10.2 %collective-permute-start.20 = (bf16[2,2,2,32,3072]{4,3,2,0,1:T(8,128)(2,1)S(1)}, bf16[2,2,2,32,3072]{4,3,2,0,1:T(8,128)(2,1)S(1)}, u32[]{:S(2)}, u32[]{:S(2)}) collective-permute-start(bf16[2,2,2,32,3072]{4,3,2,0,1:T(8,128)(2,1)S(1)} %broadcast_select_fusion), channel_id=1, source_target_pairs={{0,4},{4,0},{8,12},{12,8},{16,20},{20,16},{24,28},{28,24},{1,5},{5... | collective-permute-start | bytes 4718600 | tf_op jit(solution)/shard_map/ppermute | solution.py:24
  85.1 19.6 %collective-permute-start.10 = (bf16[1,1,4,32,3072]{4,3,2,0,1:T(8,128)(2,1)S(1)}, bf16[1,1,4,32,3072]{4,3,2,0,1:T(8,128)(2,1)S(1)}, u32[]{:S(2)}, u32[]{:S(2)}) collective-permute-start(bf16[1,1,4,32,3072]{4,3,2,0,1:T(8,128)(2,1)S(1)} %get-tuple-element.24), channel_id=1, source_target_pairs={{0,16},{4,12},{8,24},{12,4},{16,0},{20,28},{24,8},{28,20},{1,17},{... | collective-permute-start | bytes 2359304 | tf_op jit(solution)/shard_map/ppermute | solution.py:27
  87.6 20.0 %collective-permute-start.21 = (bf16[1,2,2,32,3072]{4,3,2,0,1:T(8,128)(2,1)S(1)}, bf16[1,2,2,32,3072]{4,3,2,0,1:T(8,128)(2,1)S(1)}, u32[]{:S(2)}, u32[]{:S(2)}) collective-permute-start(bf16[1,2,2,32,3072]{4,3,2,0,1:T(8,128)(2,1)S(1)} %slice.135), channel_id=1, source_target_pairs={{0,8},{4,20},{8,0},{12,28},{16,24},{20,4},{24,16},{28,12},{1,9},{5... | collective-permute-start | bytes 2359304 | tf_op jit(solution)/shard_map/ppermute | solution.py:27
  104.9 16.0 %collective-permute-start.11 = (bf16[1,2,4,32,1536]{4,3,2,0,1:T(8,128)(2,1)S(1)}, bf16[1,2,4,32,1536]{4,3,2,0,1:T(8,128)(2,1)S(1)}, u32[]{:S(2)}, u32[]{:S(2)}) collective-permute-start(bf16[1,2,4,32,1536]{4,3,2,0,1:T(8,128)(2,1)S(1)} %get-tuple-element.25), channel_id=1, source_target_pairs={{0,8},{4,20},{8,0},{12,28},{16,24},{20,4},{24,16},{28,12},{1,9},{5... | collective-permute-start | bytes 2359304 | tf_op jit(solution)/shard_map/ppermute | solution.py:27
  107.5 21.9 %collective-permute-start.13 = (bf16[1,2,4,32,1536]{4,3,2,0,1:T(8,128)(2,1)S(1)}, bf16[1,2,4,32,1536]{4,3,2,0,1:T(8,128)(2,1)S(1)}, u32[]{:S(2)}, u32[]{:S(2)}) collective-permute-start(bf16[1,2,4,32,1536]{4,3,2,0,1:T(8,128)(2,1)S(1)} %get-tuple-element.26), channel_id=1, source_target_pairs={{0,8},{4,20},{8,0},{12,28},{16,24},{20,4},{24,16},{28,12},{1,9},{5... | collective-permute-start | bytes 2359304 | tf_op jit(solution)/shard_map/ppermute | solution.py:27
  107.8 21.8 %collective-permute-start.22 = (bf16[1,1,2,32,3072]{4,3,2,0,1:T(8,128)(2,1)S(1)}, bf16[1,1,2,32,3072]{4,3,2,0,1:T(8,128)(2,1)S(1)}, u32[]{:S(2)}, u32[]{:S(2)}) collective-permute-start(bf16[1,1,2,32,3072]{4,3,2,0,1:T(8,128)(2,1)S(1)} %slice.137), channel_id=1, source_target_pairs={{0,16},{4,12},{8,24},{12,4},{16,0},{20,28},{24,8},{28,20},{1,17},{... | collective-permute-start | bytes 1179656 | tf_op jit(solution)/shard_map/ppermute | solution.py:27
  121.1 11.0 %collective-permute-start.12 = (bf16[2,2,4,32,1536]{4,3,2,0,1:T(8,128)(2,1)S(1)}, bf16[2,2,4,32,1536]{4,3,2,0,1:T(8,128)(2,1)S(1)}, u32[]{:S(2)}, u32[]{:S(2)}) collective-permute-start(bf16[2,2,4,32,1536]{4,3,2,0,1:T(8,128)(2,1)S(1)} %pad_maximum_fusion.3), channel_id=1, source_target_pairs={{0,4},{4,0},{8,12},{12,8},{16,20},{20,16},{24,28},{28,24},{1,5},{5... | collective-permute-start | bytes 4718600 | tf_op jit(solution)/shard_map/ppermute | solution.py:24
  130.5 12.1 %collective-permute-start.23 = (bf16[1,1,4,32,3072]{4,3,2,0,1:T(8,128)(2,1)S(1)}, bf16[1,1,4,32,3072]{4,3,2,0,1:T(8,128)(2,1)S(1)}, u32[]{:S(2)}, u32[]{:S(2)}) collective-permute-start(bf16[1,1,4,32,3072]{4,3,2,0,1:T(8,128)(2,1)S(1)} %fusion.45), channel_id=1, source_target_pairs={{0,16},{4,12},{8,24},{12,4},{16,0},{20,28},{24,8},{28,20},{1,17},{... | collective-permute-start | bytes 2359304 | tf_op jit(solution)/shard_map/ppermute | solution.py:27
  142.7 26.8 %collective-permute-start.24 = (bf16[1,2,4,32,1536]{4,3,2,0,1:T(8,128)(2,1)S(1)}, bf16[1,2,4,32,1536]{4,3,2,0,1:T(8,128)(2,1)S(1)}, u32[]{:S(2)}, u32[]{:S(2)}) collective-permute-start(bf16[1,2,4,32,1536]{4,3,2,0,1:T(8,128)(2,1)S(1)} %get-tuple-element.21), channel_id=1, source_target_pairs={{0,8},{4,20},{8,0},{12,28},{16,24},{20,4},{24,16},{28,12},{1,9},{5... | collective-permute-start | bytes 2359304 | tf_op jit(solution)/shard_map/ppermute | solution.py:27
  149.3 19.9 %collective-permute-start.15 = (bf16[2,2,2,32,768]{4,3,2,1,0:T(8,128)(2,1)S(1)}, bf16[2,2,2,32,768]{4,3,2,1,0:T(8,128)(2,1)S(1)}, u32[]{:S(2)}, u32[]{:S(2)}) collective-permute-start(bf16[2,2,2,32,768]{4,3,2,1,0:T(8,128)(2,1)S(1)} %slice.127), channel_id=1, source_target_pairs={{0,2},{1,3},{2,0},{3,1},{4,6},{5,7},{6,4},{7,5},{8,10},{9,11},{10,... | collective-permute-start | bytes 1179656 | tf_op jit(solution)/shard_map/ppermute | solution.py:30
  149.4 20.3 %collective-permute-start.26 = (bf16[1,2,4,32,1536]{4,3,2,0,1:T(8,128)(2,1)S(1)}, bf16[1,2,4,32,1536]{4,3,2,0,1:T(8,128)(2,1)S(1)}, u32[]{:S(2)}, u32[]{:S(2)}) collective-permute-start(bf16[1,2,4,32,1536]{4,3,2,0,1:T(8,128)(2,1)S(1)} %get-tuple-element.22), channel_id=1, source_target_pairs={{0,8},{4,20},{8,0},{12,28},{16,24},{20,4},{24,16},{28,12},{1,9},{5... | collective-permute-start | bytes 2359304 | tf_op jit(solution)/shard_map/ppermute | solution.py:27
  169.4 8.7 %collective-permute-start.16 = (bf16[2,2,1,32,768]{4,3,2,1,0:T(8,128)(2,1)S(1)}, bf16[2,2,1,32,768]{4,3,2,1,0:T(8,128)(2,1)S(1)}, u32[]{:S(2)}, u32[]{:S(2)}) collective-permute-start(bf16[2,2,1,32,768]{4,3,2,1,0:T(8,128)(2,1)S(1)} %slice.129), channel_id=1, source_target_pairs={{0,1},{1,0},{2,3},{3,2},{4,5},{5,4},{6,7},{7,6},{8,9},{9,8},{10,11... | collective-permute-start | bytes 589832 | tf_op jit(solution)/shard_map/ppermute | solution.py:30
  169.6 9.3 %collective-permute-start.25 = (bf16[2,2,4,32,1536]{4,3,2,0,1:T(8,128)(2,1)S(1)}, bf16[2,2,4,32,1536]{4,3,2,0,1:T(8,128)(2,1)S(1)}, u32[]{:S(2)}, u32[]{:S(2)}) collective-permute-start(bf16[2,2,4,32,1536]{4,3,2,0,1:T(8,128)(2,1)S(1)} %pad_maximum_fusion.6), channel_id=1, source_target_pairs={{0,4},{4,0},{8,12},{12,8},{16,20},{20,16},{24,28},{28,24},{1,5},{5... | collective-permute-start | bytes 4718600 | tf_op jit(solution)/shard_map/ppermute | solution.py:24
  169.9 9.2 %collective-permute-start.27 = (bf16[2,2,4,32,1536]{4,3,2,0,1:T(8,128)(2,1)S(1)}, bf16[2,2,4,32,1536]{4,3,2,0,1:T(8,128)(2,1)S(1)}, u32[]{:S(2)}, u32[]{:S(2)}) collective-permute-start(bf16[2,2,4,32,1536]{4,3,2,0,1:T(8,128)(2,1)S(1)} %pad_maximum_fusion.7), channel_id=1, source_target_pairs={{0,4},{4,0},{8,12},{12,8},{16,20},{20,16},{24,28},{28,24},{1,5},{5... | collective-permute-start | bytes 4718600 | tf_op jit(solution)/shard_map/ppermute | solution.py:24
  (6 other events, 29.2 us)

commit v2 on v1

--- a/solution.py
+++ b/solution.py
@@ -128,23 +128,61 @@
             return lax.concatenate([v, swap_chip(v, 0)], 0)
 
         act_all = gather(act)
-        grad_all = gather(grad)
         lead = act_all.shape[:-1]
 
         mixed = jnp.dot(flat(act_all), w_out, preferred_element_type=f32).astype(bf16).reshape(lead + (width,))
-        for bit in reversed(range(col_bits)):
-            blocks = mixed.shape[steps] // 2
-            got = swap_col(lax.slice_in_dim(mixed, blocks, 2 * blocks, axis=steps), bit)
-            keep = lax.slice_in_dim(mixed, 0, blocks, axis=steps)
-            mixed = (keep.astype(f32) + got.astype(f32)).astype(bf16)
-        mixed = flips(mixed, first, 0).reshape(tokens, width)
 
+        def halve(mixed, bit):
+            blocks = mixed.shape[steps]
+            mixed = mixed.reshape(mixed.shape[:steps] + (blocks // 2, 2) + mixed.shape[steps + 1 :])
+            return (
+                lax.index_in_dim(mixed, 0, steps + 1, False),
+                swap_col(lax.index_in_dim(mixed, 1, steps + 1, False), bit),
+            )
+
+        def merged(kept, got):
+            return (kept.astype(f32) + got.astype(f32)).astype(bf16)
+
+        plain, turned = flat(x_all), flat(turn(x_all))
+        x_rows = [
+            lax.optimization_barrier(jnp.where(core == h, plain, turned).T) for h in (0, 1)
+        ]
+        quarter = cut // 2
+
+        def weight_grad(piece, rows, half, p, into):
+            out = jnp.dot(rows, flat(piece), preferred_element_type=f32).astype(bf16)
+            return lax.dynamic_update_slice(into, out, (0, (half * 2 + p) * quarter))
+
+        own_half = core.astype(jnp.int32)
+        other_half = 1 - own_half
+        for k in reversed(range(1, steps)):
+            grad = lax.concatenate([grad, after(swap_chip(grad, k), mixed)], k)
+        near_got = swap_chip(grad[..., :quarter], 0)
+        kept, got = halve(mixed, 0)
         grad_w_out = lax.dot_general(
             flat(act_all), flat(c_all), (((0,), (0,)), ((), ())), preferred_element_type=f32
-        )
-        x_t = lax.optimization_barrier(flat(x_all).T)
-        grad_w_in = jnp.dot(x_t, flat(grad_all), preferred_element_type=f32)
-        return (mixed, grad_w_in.astype(bf16), grad_w_out.astype(bf16))
+        ).astype(bf16)
+        near_got, got, grad_w_out = lax.optimization_barrier((near_got, got, grad_w_out))
+        mixed = merged(kept, got)
+        own = [lax.concatenate([grad[..., :quarter], near_got], 0)]
+        other = [swap_core(own[0])]
+        last = after(grad[..., quarter:], near_got)
+        last_got = swap_chip(last, 0)
+        grad_w_in = weight_grad(own[0], x_rows[0], own_half, 0, jnp.zeros_like(w_in))
+        grad_w_in = weight_grad(other[0], x_rows[1], other_half, 0, grad_w_in)
+        for bit in range(1, col_bits):
+            kept, got = halve(mixed, bit)
+            if bit + 1 < col_bits:
+                mixed = merged(kept, got)
+        own.append(lax.concatenate([last, after(last_got, grad_w_in)], 0))
+        other.append(swap_core(own[1]))
+        grad_w_in = weight_grad(own[1], x_rows[0], own_half, 1, grad_w_in)
+        if col_bits > 1:
+            got = after(got, grad_w_in)
+            mixed = merged(kept, got)
+        mixed = flips(mixed, first, 0).reshape(tokens, width)
+        grad_w_in = weight_grad(after(other[1], got), x_rows[1], other_half, 1, grad_w_in)
+        return (mixed, grad_w_in, grad_w_out)
 
     return per_device
 

time: 193 us -> 195 us (1.010)
  waiting for transfers between devices: 104 us -> 93.1 us
  local copies, waits for them, and re-layouts: 3.48 us -> 12.8 us
  other arithmetic: 22.2 us -> 17.8 us
  starting transfers between devices: 27.2 us -> 31.1 us
  matrix products: 34.4 us -> 38.1 us
    ppermute x6, waiting for transfers between devices: 46.1 us -> 36.8 us  [swap_col(): return lax.ppermute(v, 'col', [(i, i ^ 1 << bit) for i in range(n_col)])]
    concatenate x2 -> x1, other arithmetic: 11.1 us -> 5.46 us  [gather(): lax.concatenate(firsts + seconds, steps + 2)]
    broadcast_in_dim x0 -> x1, local copies, waits for them, and re-layouts: none -> 4.91 us  [per_device(): jnp.zeros_like(w_in)]
    ppermute x6, starting transfers between devices: 6.45 us -> 10.4 us  [swap_col(): return lax.ppermute(v, 'col', [(i, i ^ 1 << bit) for i in range(n_col)])]
    dot_general x1 -> x4, matrix products: 7.58 us -> 11.3 us  [weight_grad(): out = jnp.dot(rows, flat(piece), preferred_element_type=f32).astype(bf16)]
    unnamed x4 -> x20, local copies, waits for them, and re-layouts: 3.12 us -> 5.55 us
    ppermute x14, waiting for transfers between devices: 55.7 us -> 53.4 us  [swap_chip(): lax.ppermute(v, 'row', [(i, i ^ 1 << orders[i & 1][step]) for i in range(...]
  transfers between devices with their start and end apart: 28 -> 28, of which waited for: 13 -> 14; matrix products, arithmetic and copies ran while one was open for 20% -> 30% of each run, Pallas kernels for 0% -> 0%
where the time goes in v2:
time: 195 us; the launch traced here: 194 us
  waiting for transfers between devices  93.1 us (48%)
  matrix products  38.1 us (20%)
  starting transfers between devices  31.1 us (16%)
  other arithmetic  17.8 us (9%)
  local copies, waits for them, and re-layouts  12.8 us (7%)
    ppermute x14, waiting for transfers between devices, swap_chip(): lax.ppermute(v, 'row', [(i, i ^ 1 << orders[i & 1][step]) for i in range(...  53.4 us
    ppermute x6, waiting for transfers between devices, swap_col(): return lax.ppermute(v, 'col', [(i, i ^ 1 << bit) for i in range(n_col)])  36.8 us
    ppermute x14, starting transfers between devices, swap_chip(): lax.ppermute(v, 'row', [(i, i ^ 1 << orders[i & 1][step]) for i in range(...  19.3 us
    dot_general x4, matrix products, weight_grad(): out = jnp.dot(rows, flat(piece), preferred_element_type=f32).astype(bf16)  11.3 us
    ppermute x6, starting transfers between devices, swap_col(): return lax.ppermute(v, 'col', [(i, i ^ 1 << bit) for i in range(n_col)])  10.4 us
    dot_general x4, matrix products, up(): jnp.dot(flat(x), w_in[:, h], preferred_element_type=f32)  8.07 us
    dot_general x1, matrix products, per_device(): lax.dot_general(flat(act_all), flat(c_all), (((0,), (0,)), ((), ())), pre...  7.63 us
    dot_general x4, matrix products, back(): lax.dot_general(flat(c), w_out[h], (((1,), (1,)), ((), ())), preferred_el...  5.95 us
  transfers between devices with their start and end apart: 28, of which 14 were waited for; matrix products, arithmetic and copies ran while one was open for 30% of the time, Pallas kernels for 0%

profile of v2, /device:TPU:0, one launch (start us, length us, event | category | flops | bytes accessed | tf_op | source)
XLA Modules:
  0.0 194.2 jit_solution(11273457311282074202)
XLA Ops:
  1.8 3.1 %collective-permute-start = (bf16[2,2,1,32,768]{4,3,2,1,0:T(8,128)(2,1)S(1)}, bf16[2,2,1,32,768]{4,3,2,1,0:T(8,128)(2,1)S(1)}, u32[]{:S(2)}, u32[]{:S(2)}) collective-permute-start(bf16[2,2,1,32,768]{4,3,2,1,0:T(8,128)(2,1)S(1)} %reverse_select_fusion.4), channel_id=1, source_target_pairs={{0,1},{1,0},{2,3},{3,2},{4,5},{5,4},{6,7},{7,6},{8,9},{9,8},{10,11... | collective-permute-start | bytes 589832 | tf_op jit(solution)/shard_map/ppermute | solution.py:30
  6.0 4.5 %collective-permute-done = bf16[2,2,1,32,768]{4,3,2,1,0:T(8,128)(2,1)S(1)} collective-permute-done((bf16[2,2,1,32,768]{4,3,2,1,0:T(8,128)(2,1)S(1)}, bf16[2,2,1,32,768]{4,3,2,1,0:T(8,128)(2,1)S(1)}, u32[]{:S(2)}, u32[]{:S(2)}) %collective-permute-start) | collective-permute-done | bytes 196640 | tf_op jit(solution)/shard_map/ppermute | solution.py:30
  10.6 3.9 %fusion.22 = bf16[256,3072]{1,0:T(8,128)(2,1)S(1)} fusion(bf16[256,768]{1,0:T(8,128)(2,1)S(1)} %bitcast.113, bf16[768,6144]{1,0:T(8,128)(2,1)} %param.5), kind=kOutput, calls=%fused_computation.20 | convolution fusion | flops 1208745984 | bytes 6684672 | tf_op jit(solution)/shard_map/dot_general | solution.py:86
  17.4 2.0 %copy-done.8 = bf16[6144,768]{1,0:T(8,128)(2,1)S(1)} copy-done((bf16[6144,768]{1,0:T(8,128)(2,1)S(1)}, bf16[6144,768]{1,0:T(8,128)(2,1)}, u32[]{:S(2)}) %copy-start.8) | copy-done | bytes 9437208
  22.5 3.1 %collective-permute-start.4 = (bf16[2,2,2,32,768]{4,3,2,1,0:T(8,128)(2,1)S(1)}, bf16[2,2,2,32,768]{4,3,2,1,0:T(8,128)(2,1)S(1)}, u32[]{:S(2)}, u32[]{:S(2)}) collective-permute-start(bf16[2,2,2,32,768]{4,3,2,1,0:T(8,128)(2,1)S(1)} %pad_maximum_fusion.9), channel_id=1, source_target_pairs={{0,2},{1,3},{2,0},{3,1},{4,6},{5,7},{6,4},{7,5},{8,10},{9,11},{10,... | collective-permute-start | bytes 1179656 | tf_op jit(solution)/shard_map/ppermute | solution.py:30
  28.9 14.9 %collective-permute-done.4 = bf16[2,2,2,32,768]{4,3,2,1,0:T(8,128)(2,1)S(1)} collective-permute-done((bf16[2,2,2,32,768]{4,3,2,1,0:T(8,128)(2,1)S(1)}, bf16[2,2,2,32,768]{4,3,2,1,0:T(8,128)(2,1)S(1)}, u32[]{:S(2)}, u32[]{:S(2)}) %collective-permute-start.4) | collective-permute-done | bytes 393248 | tf_op jit(solution)/shard_map/ppermute | solution.py:30
  54.5 7.8 %collective-permute-done.15 = bf16[1,2,2,32,3072]{4,3,2,0,1:T(8,128)(2,1)S(1)} collective-permute-done((bf16[1,2,2,32,3072]{4,3,2,0,1:T(8,128)(2,1)S(1)}, bf16[1,2,2,32,3072]{4,3,2,0,1:T(8,128)(2,1)S(1)}, u32[]{:S(2)}, u32[]{:S(2)}) %collective-permute-start.15) | collective-permute-done | bytes 786464 | tf_op jit(solution)/shard_map/ppermute | solution.py:27
  62.6 2.5 %collective-permute-start.16 = (bf16[1,1,2,32,3072]{4,3,2,0,1:T(8,128)(2,1)S(1)}, bf16[1,1,2,32,3072]{4,3,2,0,1:T(8,128)(2,1)S(1)}, u32[]{:S(2)}, u32[]{:S(2)}) collective-permute-start(bf16[1,1,2,32,3072]{4,3,2,0,1:T(8,128)(2,1)S(1)} %slice.131), channel_id=1, source_target_pairs={{0,16},{4,12},{8,24},{12,4},{16,0},{20,28},{24,8},{28,20},{1,17},{... | collective-permute-start | bytes 1179656 | tf_op jit(solution)/shard_map/ppermute | solution.py:27
  65.0 9.4 %collective-permute-done.17 = bf16[2,2,2,32,768]{4,3,2,1,0:T(8,128)(2,1)S(1)} collective-permute-done((bf16[2,2,2,32,768]{4,3,2,1,0:T(8,128)(2,1)S(1)}, bf16[2,2,2,32,768]{4,3,2,1,0:T(8,128)(2,1)S(1)}, u32[]{:S(2)}, u32[]{:S(2)}) %collective-permute-start.17) | collective-permute-done | bytes 393248 | tf_op jit(solution)/shard_map/ppermute | solution.py:30
  81.1 5.8 %collective-permute-done.9 = bf16[1,1,2,32,3072]{4,3,2,0,1:T(8,128)(2,1)S(1)} collective-permute-done((bf16[1,1,2,32,3072]{4,3,2,0,1:T(8,128)(2,1)S(1)}, bf16[1,1,2,32,3072]{4,3,2,0,1:T(8,128)(2,1)S(1)}, u32[]{:S(2)}, u32[]{:S(2)}) %collective-permute-start.9) | collective-permute-done | bytes 393248 | tf_op jit(solution)/shard_map/ppermute | solution.py:27
  91.5 16.4 %collective-permute-done.10 = bf16[1,1,4,32,3072]{4,3,2,0,1:T(8,128)(2,1)S(1)} collective-permute-done((bf16[1,1,4,32,3072]{4,3,2,0,1:T(8,128)(2,1)S(1)}, bf16[1,1,4,32,3072]{4,3,2,0,1:T(8,128)(2,1)S(1)}, u32[]{:S(2)}, u32[]{:S(2)}) %collective-permute-start.10) | collective-permute-done | bytes 786464 | tf_op jit(solution)/shard_map/ppermute | solution.py:27
  112.2 11.3 %collective-permute-done.13 = bf16[1,2,4,32,1536]{4,3,2,0,1:T(8,128)(2,1)S(1)} collective-permute-done((bf16[1,2,4,32,1536]{4,3,2,0,1:T(8,128)(2,1)S(1)}, bf16[1,2,4,32,1536]{4,3,2,0,1:T(8,128)(2,1)S(1)}, u32[]{:S(2)}, u32[]{:S(2)}) %collective-permute-start.13) | collective-permute-done | bytes 786464 | tf_op jit(solution)/shard_map/ppermute | solution.py:27
  123.7 8.2 %collective-permute-done.11 = bf16[1,2,4,32,1536]{4,3,2,0,1:T(8,128)(2,1)S(1)} collective-permute-done((bf16[1,2,4,32,1536]{4,3,2,0,1:T(8,128)(2,1)S(1)}, bf16[1,2,4,32,1536]{4,3,2,0,1:T(8,128)(2,1)S(1)}, u32[]{:S(2)}, u32[]{:S(2)}) %collective-permute-start.11) | collective-permute-done | bytes 786464 | tf_op jit(solution)/shard_map/ppermute | solution.py:27
  135.8 5.5 %pad_maximum_fusion = bf16[2,2,4,32,6144]{4,3,2,1,0:T(8,128)(2,1)S(1)} fusion(bf16[2,2,4,32,1536]{4,3,2,1,0:T(8,128)(2,1)S(1)} %get-tuple-element.30, bf16[2,2,4,32,1536]{4,3,2,1,0:T(8,128)(2,1)S(1)} %get-tuple-element.28, bf16[2,2,4,32,1536]{4,3,2,0,1:T(8,128)(2,1)S(1)} %get-tuple-element.27, bf16[2,2,4,32,1536]{4,3,2,0,1:T(8,128)(2,1)S(1)} %get-tuple-element.29), kind=kLoop, calls=%fused_computation.1 | loop fusion | flops 25165824 | bytes 12582912 | tf_op jit(solution)/shard_map/concatenate | solution.py:125
  141.3 5.1 %convolution_convert_fusion.4 = bf16[512,768]{1,0:T(8,128)(2,1)S(1)} fusion(bf16[512,6144]{1,0:T(8,128)(2,1)S(1)} %bitcast.85, bf16[6144,768]{1,0:T(8,128)(2,1)S(1)} %copy-done.8), kind=kOutput, calls=%fused_computation.67 | convolution fusion | flops 4832231424 | bytes 16515072 | tf_op jit(solution)/shard_map/dot_general | solution.py:133
  148.4 7.6 %bitcast_convert_fusion = bf16[6144,768]{1,0:T(8,128)(2,1)} fusion(bf16[2,2,4,32,6144]{4,3,2,1,0:T(8,128)(2,1)S(1)} %pad_maximum_fusion, bf16[2,2,2,32,768]{4,3,2,1,0:T(8,128)(2,1)S(1)} %collective-permute-done.17, bf16[2,2,2,32,768]{4,3,2,1,0:T(8,128)(2,1)S(1)} %pad_maximum_fusion.10), kind=kOutput, calls=%fused_computation | convolution fusion | flops 4836950016 | bytes 16515072 | tf_op jit(solution)/shard_map/dot_general | solution.py:162
  157.7 2.4 %collective-permute-done.22 = bf16[1,2,4,32,1536]{4,3,2,0,1:T(8,128)(2,1)S(1)} collective-permute-done((bf16[1,2,4,32,1536]{4,3,2,0,1:T(8,128)(2,1)S(1)}, bf16[1,2,4,32,1536]{4,3,2,0,1:T(8,128)(2,1)S(1)}, u32[]{:S(2)}, u32[]{:S(2)}) %collective-permute-start.22) | collective-permute-done | bytes 786464 | tf_op jit(solution)/shard_map/ppermute | solution.py:27
  162.5 4.9 %broadcast_in_dim.3 = bf16[768,6144]{1,0:T(8,128)(2,1)} broadcast(bf16[]{:T(256)} %constant.27.clone.1), dimensions={} | broadcast | bytes 9437186 | tf_op jit(solution)/shard_map/broadcast_in_dim | solution.py:171
  167.4 2.8 %fusion.43 = bf16[768,6144]{1,0:T(8,128)(2,1)} fusion(bf16[768,6144]{1,0:T(8,128)(2,1)} %broadcast_in_dim.3, s32[]{:T(128)S(6)} %select_n.141, bf16[768,512]{0,1:T(8,128)(2,1)S(1)} %bitcast.109, bf16[512,1536]{1,0:T(8,128)(2,1)S(1)} %bitcast.103), kind=kOutput, calls=%fused_computation.33 | convolution fusion | flops 1209139200 | bytes 4718596 | tf_op jit(solution)/shard_map/dot_general | solution.py:153
  171.8 2.8 %fusion.42 = bf16[768,6144]{1,0:T(8,128)(2,1)} fusion(bf16[768,6144]{1,0:T(8,128)(2,1)} %fusion.43, s32[]{:T(128)S(6)} %select_n.145, bf16[768,512]{0,1:T(8,128)(2,1)S(1)} %bitcast.107, bf16[512,1536]{1,0:T(8,128)(2,1)S(1)} %bitcast.104), kind=kOutput, calls=%fused_computation.31 | convolution fusion | flops 1209139200 | bytes 4718596 | tf_op jit(solution)/shard_map/dot_general | solution.py:153
  176.7 3.4 %collective-permute-start.24 = (bf16[2,2,1,32,768]{4,3,2,1,0:T(8,128)(2,1)S(1)}, bf16[2,2,1,32,768]{4,3,2,1,0:T(8,128)(2,1)S(1)}, u32[]{:S(2)}, u32[]{:S(2)}) collective-permute-start(bf16[2,2,1,32,768]{4,3,2,1,0:T(8,128)(2,1)S(1)} %slice_bitcast_fusion), channel_id=1, source_target_pairs={{0,2},{1,3},{2,0},{3,1},{4,6},{5,7},{6,4},{7,5},{8,10},{9,11},{10,... | collective-permute-start | bytes 589832 | tf_op jit(solution)/shard_map/ppermute | solution.py:30
  180.2 2.8 %fusion.41 = bf16[768,6144]{1,0:T(8,128)(2,1)} fusion(bf16[768,6144]{1,0:T(8,128)(2,1)} %fusion.42, s32[]{:T(128)S(6)} %select_n.146, bf16[768,512]{0,1:T(8,128)(2,1)S(1)} %bitcast.110, bf16[512,1536]{1,0:T(8,128)(2,1)S(1)} %bitcast.105), kind=kOutput, calls=%fused_computation.29 | convolution fusion | flops 1209139200 | bytes 4718596 | tf_op jit(solution)/shard_map/dot_general | solution.py:153
  183.1 6.3 %collective-permute-done.24 = bf16[2,2,1,32,768]{4,3,2,1,0:T(8,128)(2,1)S(1)} collective-permute-done((bf16[2,2,1,32,768]{4,3,2,1,0:T(8,128)(2,1)S(1)}, bf16[2,2,1,32,768]{4,3,2,1,0:T(8,128)(2,1)S(1)}, u32[]{:S(2)}, u32[]{:S(2)}) %collective-permute-start.24) | collective-permute-done | bytes 196640 | tf_op jit(solution)/shard_map/ppermute | solution.py:30
  191.3 2.8 %fusion.40 = bf16[768,6144]{1,0:T(8,128)(2,1)} fusion(bf16[768,6144]{1,0:T(8,128)(2,1)} %fusion.41, s32[]{:T(128)S(6)} %select_n.149, bf16[768,512]{0,1:T(8,128)(2,1)S(1)} %bitcast.108, bf16[512,1536]{1,0:T(8,128)(2,1)S(1)} %bitcast.102), kind=kOutput, calls=%fused_computation.27 | convolution fusion | flops 1209139200 | bytes 4718596 | tf_op jit(solution)/shard_map/dot_general | solution.py:153
  (121 shorter events, 53.3 us)
Async XLA Ops:
  1.8 8.8 %collective-permute-start = (bf16[2,2,1,32,768]{4,3,2,1,0:T(8,128)(2,1)S(1)}, bf16[2,2,1,32,768]{4,3,2,1,0:T(8,128)(2,1)S(1)}, u32[]{:S(2)}, u32[]{:S(2)}) collective-permute-start(bf16[2,2,1,32,768]{4,3,2,1,0:T(8,128)(2,1)S(1)} %reverse_select_fusion.4), channel_id=1, source_target_pairs={{0,1},{1,0},{2,3},{3,2},{4,5},{5,4},{6,7},{7,6},{8,9},{9,8},{10,11... | collective-permute-start | bytes 589832 | tf_op jit(solution)/shard_map/ppermute | solution.py:30
  6.0 11.4 %collective-permute-start.5 = (bf16[2,2,1,32,768]{4,3,2,1,0:T(8,128)(2,1)S(1)}, bf16[2,2,1,32,768]{4,3,2,1,0:T(8,128)(2,1)S(1)}, u32[]{:S(2)}, u32[]{:S(2)}) collective-permute-start(bf16[2,2,1,32,768]{4,3,2,1,0:T(8,128)(2,1)S(1)} %reverse_select_fusion.2), channel_id=1, source_target_pairs={{0,1},{1,0},{2,3},{3,2},{4,5},{5,4},{6,7},{7,6},{8,9},{9,8},{10,11... | collective-permute-start | bytes 589832 | tf_op jit(solution)/shard_map/ppermute | solution.py:30
  17.2 8.4 %collective-permute-start.1 = (bf16[2,2,2,32,3072]{4,3,2,0,1:T(8,128)(2,1)S(1)}, bf16[2,2,2,32,3072]{4,3,2,0,1:T(8,128)(2,1)S(1)}, u32[]{:S(2)}, u32[]{:S(2)}) collective-permute-start(bf16[2,2,2,32,3072]{4,3,2,0,1:T(8,128)(2,1)S(1)} %broadcast_select_fusion.3), channel_id=1, source_target_pairs={{0,4},{4,0},{8,12},{12,8},{16,20},{20,16},{24,28},{28,24},{1,5},{5... | collective-permute-start | bytes 4718600 | tf_op jit(solution)/shard_map/ppermute | solution.py:24
  22.5 21.3 %collective-permute-start.4 = (bf16[2,2,2,32,768]{4,3,2,1,0:T(8,128)(2,1)S(1)}, bf16[2,2,2,32,768]{4,3,2,1,0:T(8,128)(2,1)S(1)}, u32[]{:S(2)}, u32[]{:S(2)}) collective-permute-start(bf16[2,2,2,32,768]{4,3,2,1,0:T(8,128)(2,1)S(1)} %pad_maximum_fusion.9), channel_id=1, source_target_pairs={{0,2},{1,3},{2,0},{3,1},{4,6},{5,7},{6,4},{7,5},{8,10},{9,11},{10,... | collective-permute-start | bytes 1179656 | tf_op jit(solution)/shard_map/ppermute | solution.py:30
  26.5 17.2 %collective-permute-start.2 = (bf16[1,2,2,32,3072]{4,3,2,0,1:T(8,128)(2,1)S(1)}, bf16[1,2,2,32,3072]{4,3,2,0,1:T(8,128)(2,1)S(1)}, u32[]{:S(2)}, u32[]{:S(2)}) collective-permute-start(bf16[1,2,2,32,3072]{4,3,2,0,1:T(8,128)(2,1)S(1)} %slice.118), channel_id=1, source_target_pairs={{0,8},{4,20},{8,0},{12,28},{16,24},{20,4},{24,16},{28,12},{1,9},{5... | collective-permute-start | bytes 2359304 | tf_op jit(solution)/shard_map/ppermute | solution.py:27
  46.9 15.5 %collective-permute-start.15 = (bf16[1,2,2,32,3072]{4,3,2,0,1:T(8,128)(2,1)S(1)}, bf16[1,2,2,32,3072]{4,3,2,0,1:T(8,128)(2,1)S(1)}, u32[]{:S(2)}, u32[]{:S(2)}) collective-permute-start(bf16[1,2,2,32,3072]{4,3,2,0,1:T(8,128)(2,1)S(1)} %slice.129), channel_id=1, source_target_pairs={{0,8},{4,20},{8,0},{12,28},{16,24},{20,4},{24,16},{28,12},{1,9},{5... | collective-permute-start | bytes 2359304 | tf_op jit(solution)/shard_map/ppermute | solution.py:27
  51.1 24.7 %collective-permute-start.8 = (bf16[1,2,2,32,3072]{4,3,2,0,1:T(8,128)(2,1)S(1)}, bf16[1,2,2,32,3072]{4,3,2,0,1:T(8,128)(2,1)S(1)}, u32[]{:S(2)}, u32[]{:S(2)}) collective-permute-start(bf16[1,2,2,32,3072]{4,3,2,0,1:T(8,128)(2,1)S(1)} %slice.122), channel_id=1, source_target_pairs={{0,8},{4,20},{8,0},{12,28},{16,24},{20,4},{24,16},{28,12},{1,9},{5... | collective-permute-start | bytes 2359304 | tf_op jit(solution)/shard_map/ppermute | solution.py:27
  52.9 28.1 %collective-permute-start.3 = (bf16[1,1,2,32,3072]{4,3,2,0,1:T(8,128)(2,1)S(1)}, bf16[1,1,2,32,3072]{4,3,2,0,1:T(8,128)(2,1)S(1)}, u32[]{:S(2)}, u32[]{:S(2)}) collective-permute-start(bf16[1,1,2,32,3072]{4,3,2,0,1:T(8,128)(2,1)S(1)} %slice.120), channel_id=1, source_target_pairs={{0,16},{4,12},{8,24},{12,4},{16,0},{20,28},{24,8},{28,20},{1,17},{... | collective-permute-start | bytes 1179656 | tf_op jit(solution)/shard_map/ppermute | solution.py:27
  54.5 19.9 %collective-permute-start.17 = (bf16[2,2,2,32,768]{4,3,2,1,0:T(8,128)(2,1)S(1)}, bf16[2,2,2,32,768]{4,3,2,1,0:T(8,128)(2,1)S(1)}, u32[]{:S(2)}, u32[]{:S(2)}) collective-permute-start(bf16[2,2,2,32,768]{4,3,2,1,0:T(8,128)(2,1)S(1)} %pad_maximum_fusion.10), channel_id=1, source_target_pairs={{0,2},{1,3},{2,0},{3,1},{4,6},{5,7},{6,4},{7,5},{8,10},{9,11},{10,... | collective-permute-start | bytes 1179656 | tf_op jit(solution)/shard_map/ppermute | solution.py:30
  62.6 47.1 %collective-permute-start.16 = (bf16[1,1,2,32,3072]{4,3,2,0,1:T(8,128)(2,1)S(1)}, bf16[1,1,2,32,3072]{4,3,2,0,1:T(8,128)(2,1)S(1)}, u32[]{:S(2)}, u32[]{:S(2)}) collective-permute-start(bf16[1,1,2,32,3072]{4,3,2,0,1:T(8,128)(2,1)S(1)} %slice.131), channel_id=1, source_target_pairs={{0,16},{4,12},{8,24},{12,4},{16,0},{20,28},{24,8},{28,20},{1,17},{... | collective-permute-start | bytes 1179656 | tf_op jit(solution)/shard_map/ppermute | solution.py:27
  80.9 8.1 %collective-permute-start.18 = (bf16[2,2,2,32,3072]{4,3,2,0,1:T(8,128)(2,1)S(1)}, bf16[2,2,2,32,3072]{4,3,2,0,1:T(8,128)(2,1)S(1)}, u32[]{:S(2)}, u32[]{:S(2)}) collective-permute-start(bf16[2,2,2,32,3072]{4,3,2,0,1:T(8,128)(2,1)S(1)} %broadcast_select_fusion), channel_id=1, source_target_pairs={{0,4},{4,0},{8,12},{12,8},{16,20},{20,16},{24,28},{28,24},{1,5},{5... | collective-permute-start | bytes 4718600 | tf_op jit(solution)/shard_map/ppermute | solution.py:24
  87.4 20.5 %collective-permute-start.10 = (bf16[1,1,4,32,3072]{4,3,2,0,1:T(8,128)(2,1)S(1)}, bf16[1,1,4,32,3072]{4,3,2,0,1:T(8,128)(2,1)S(1)}, u32[]{:S(2)}, u32[]{:S(2)}) collective-permute-start(bf16[1,1,4,32,3072]{4,3,2,0,1:T(8,128)(2,1)S(1)} %get-tuple-element.35), channel_id=1, source_target_pairs={{0,16},{4,12},{8,24},{12,4},{16,0},{20,28},{24,8},{28,20},{1,17},{... | collective-permute-start | bytes 2359304 | tf_op jit(solution)/shard_map/ppermute | solution.py:27
  89.9 20.4 %collective-permute-start.19 = (bf16[1,2,2,32,3072]{4,3,2,0,1:T(8,128)(2,1)S(1)}, bf16[1,2,2,32,3072]{4,3,2,0,1:T(8,128)(2,1)S(1)}, u32[]{:S(2)}, u32[]{:S(2)}) collective-permute-start(bf16[1,2,2,32,3072]{4,3,2,0,1:T(8,128)(2,1)S(1)} %slice.133), channel_id=1, source_target_pairs={{0,8},{4,20},{8,0},{12,28},{16,24},{20,4},{24,16},{28,12},{1,9},{5... | collective-permute-start | bytes 2359304 | tf_op jit(solution)/shard_map/ppermute | solution.py:27
  108.0 15.5 %collective-permute-start.13 = (bf16[1,2,4,32,1536]{4,3,2,0,1:T(8,128)(2,1)S(1)}, bf16[1,2,4,32,1536]{4,3,2,0,1:T(8,128)(2,1)S(1)}, u32[]{:S(2)}, u32[]{:S(2)}) collective-permute-start(bf16[1,2,4,32,1536]{4,3,2,0,1:T(8,128)(2,1)S(1)} %get-tuple-element.34), channel_id=1, source_target_pairs={{0,8},{4,20},{8,0},{12,28},{16,24},{20,4},{24,16},{28,12},{1,9},{5... | collective-permute-start | bytes 2359304 | tf_op jit(solution)/shard_map/ppermute | solution.py:27
  109.8 22.2 %collective-permute-start.11 = (bf16[1,2,4,32,1536]{4,3,2,0,1:T(8,128)(2,1)S(1)}, bf16[1,2,4,32,1536]{4,3,2,0,1:T(8,128)(2,1)S(1)}, u32[]{:S(2)}, u32[]{:S(2)}) collective-permute-start(bf16[1,2,4,32,1536]{4,3,2,0,1:T(8,128)(2,1)S(1)} %get-tuple-element.33), channel_id=1, source_target_pairs={{0,8},{4,20},{8,0},{12,28},{16,24},{20,4},{24,16},{28,12},{1,9},{5... | collective-permute-start | bytes 2359304 | tf_op jit(solution)/shard_map/ppermute | solution.py:27
  110.5 21.7 %collective-permute-start.20 = (bf16[1,1,2,32,3072]{4,3,2,0,1:T(8,128)(2,1)S(1)}, bf16[1,1,2,32,3072]{4,3,2,0,1:T(8,128)(2,1)S(1)}, u32[]{:S(2)}, u32[]{:S(2)}) collective-permute-start(bf16[1,1,2,32,3072]{4,3,2,0,1:T(8,128)(2,1)S(1)} %slice.135), channel_id=1, source_target_pairs={{0,16},{4,12},{8,24},{12,4},{16,0},{20,28},{24,8},{28,20},{1,17},{... | collective-permute-start | bytes 1179656 | tf_op jit(solution)/shard_map/ppermute | solution.py:27
  123.7 10.5 %collective-permute-start.14 = (bf16[2,2,4,32,1536]{4,3,2,0,1:T(8,128)(2,1)S(1)}, bf16[2,2,4,32,1536]{4,3,2,0,1:T(8,128)(2,1)S(1)}, u32[]{:S(2)}, u32[]{:S(2)}) collective-permute-start(bf16[2,2,4,32,1536]{4,3,2,0,1:T(8,128)(2,1)S(1)} %pad_maximum_fusion.3), channel_id=1, source_target_pairs={{0,4},{4,0},{8,12},{12,8},{16,20},{20,16},{24,28},{28,24},{1,5},{5... | collective-permute-start | bytes 4718600 | tf_op jit(solution)/shard_map/ppermute | solution.py:24
  133.0 14.1 %collective-permute-start.21 = (bf16[1,1,4,32,3072]{4,3,2,0,1:T(8,128)(2,1)S(1)}, bf16[1,1,4,32,3072]{4,3,2,0,1:T(8,128)(2,1)S(1)}, u32[]{:S(2)}, u32[]{:S(2)}) collective-permute-start(bf16[1,1,4,32,3072]{4,3,2,0,1:T(8,128)(2,1)S(1)} %fusion.49), channel_id=1, source_target_pairs={{0,16},{4,12},{8,24},{12,4},{16,0},{20,28},{24,8},{28,20},{1,17},{... | collective-permute-start | bytes 2359304 | tf_op jit(solution)/shard_map/ppermute | solution.py:27
  146.5 11.2 %collective-permute-start.23 = (bf16[2,2,2,32,768]{4,3,1,0,2:T(8,128)(2,1)S(1)}, bf16[2,2,2,32,768]{4,3,1,0,2:T(8,128)(2,1)S(1)}, u32[]{:S(2)}, u32[]{:S(2)}) collective-permute-start(bf16[2,2,2,32,768]{4,3,1,0,2:T(8,128)(2,1)S(1)} %bitcast.115), channel_id=1, source_target_pairs={{0,1},{1,0},{2,3},{3,2},{4,5},{5,4},{6,7},{7,6},{8,9},{9,8},{10,11... | collective-permute-start | bytes 1179656 | tf_op jit(solution)/shard_map/ppermute | solution.py:30
  148.2 12.0 %collective-permute-start.22 = (bf16[1,2,4,32,1536]{4,3,2,0,1:T(8,128)(2,1)S(1)}, bf16[1,2,4,32,1536]{4,3,2,0,1:T(8,128)(2,1)S(1)}, u32[]{:S(2)}, u32[]{:S(2)}) collective-permute-start(bf16[1,2,4,32,1536]{4,3,2,0,1:T(8,128)(2,1)S(1)} %get-tuple-element.32), channel_id=1, source_target_pairs={{0,8},{4,20},{8,0},{12,28},{16,24},{20,4},{24,16},{28,12},{1,9},{5... | collective-permute-start | bytes 2359304 | tf_op jit(solution)/shard_map/ppermute | solution.py:27
  160.3 9.9 %collective-permute-start.25 = (bf16[2,2,4,32,1536]{4,3,2,0,1:T(8,128)(2,1)S(1)}, bf16[2,2,4,32,1536]{4,3,2,0,1:T(8,128)(2,1)}, u32[]{:S(2)}, u32[]{:S(2)}) collective-permute-start(bf16[2,2,4,32,1536]{4,3,2,0,1:T(8,128)(2,1)S(1)} %pad_maximum_fusion.5), channel_id=1, source_target_pairs={{0,4},{4,0},{8,12},{12,8},{16,20},{20,16},{24,28},{28,24},{1,5},{5... | collective-permute-start | bytes 4718600 | tf_op jit(solution)/shard_map/ppermute | solution.py:24
  160.6 14.0 %collective-permute-start.26 = (bf16[1,2,4,32,1536]{4,3,2,0,1:T(8,128)(2,1)}, bf16[1,2,4,32,1536]{4,3,2,0,1:T(8,128)(2,1)S(1)}, u32[]{:S(2)}, u32[]{:S(2)}) collective-permute-start(bf16[1,2,4,32,1536]{4,3,2,0,1:T(8,128)(2,1)} %get-tuple-element.22), channel_id=1, source_target_pairs={{0,8},{4,20},{8,0},{12,28},{16,24},{20,4},{24,16},{28,12},{1,9},{5... | collective-permute-start | bytes 2359304 | tf_op jit(solution)/shard_map/ppermute | solution.py:27
  174.7 15.5 %collective-permute-start.27 = (bf16[2,2,4,32,1536]{4,3,2,0,1:T(8,128)(2,1)S(1)}, bf16[2,2,4,32,1536]{4,3,2,0,1:T(8,128)(2,1)S(1)}, u32[]{:S(2)}, u32[]{:S(2)}) collective-permute-start(bf16[2,2,4,32,1536]{4,3,2,0,1:T(8,128)(2,1)S(1)} %constant_dynamic-update-slice_fusion), channel_id=1, source_target_pairs={{0,4},{4,0},{8,12},{12,8},{16,20},{20,16},{24,28},{28,24},{1,5},{5... | collective-permute-start | bytes 4718600 | tf_op jit(solution)/shard_map/ppermute | solution.py:24
  176.7 12.7 %collective-permute-start.24 = (bf16[2,2,1,32,768]{4,3,2,1,0:T(8,128)(2,1)S(1)}, bf16[2,2,1,32,768]{4,3,2,1,0:T(8,128)(2,1)S(1)}, u32[]{:S(2)}, u32[]{:S(2)}) collective-permute-start(bf16[2,2,1,32,768]{4,3,2,1,0:T(8,128)(2,1)S(1)} %slice_bitcast_fusion), channel_id=1, source_target_pairs={{0,2},{1,3},{2,0},{3,1},{4,6},{5,7},{6,4},{7,5},{8,10},{9,11},{10,... | collective-permute-start | bytes 589832 | tf_op jit(solution)/shard_map/ppermute | solution.py:30
  (13 other events, 60.2 us)

commit v3 on v2

--- a/solution.py
+++ b/solution.py
@@ -66,11 +66,6 @@
                 v = v.astype(bf16)
         return v, seen
 
-    def gather_chips(v, stop):
-        for k in reversed(range(stop, steps)):
-            v = lax.concatenate([v, swap_chip(v, k)], k)
-        return v
-
     def per_device(latents, w_in, w_out, cotangent):
         tokens, width = latents.shape
         cut = w_in.shape[1] // 2
@@ -113,21 +108,25 @@
         hid, grad = lax.optimization_barrier((hid, grad))
         grad = (grad * gelu_parts(hid)[1]).astype(bf16)
 
-        def gather(v):
-            v = gather_chips(v, 1)
+        def gather(v, room):
             quarter = cut // 2
             firsts, seconds = [], []
             for p in range(2):
-                w = gather_chips_last(v[..., p * quarter : (p + 1) * quarter])
+                w = v[..., p * quarter : (p + 1) * quarter]
+                got = swap_chip(w, 0)
+                if p == 1:
+                    got, room = lax.optimization_barrier((got, room))
+                w = lax.concatenate([w, got], 0)
                 got = swap_core(w)
                 firsts.append(jnp.where(core == 0, w, got))
                 seconds.append(turn(jnp.where(core == 0, got, w)))
-            return lax.optimization_barrier(lax.concatenate(firsts + seconds, steps + 2))
+            return lax.optimization_barrier(lax.concatenate(firsts + seconds, steps + 2)), room
 
-        def gather_chips_last(v):
-            return lax.concatenate([v, swap_chip(v, 0)], 0)
-
-        act_all = gather(act)
+        for k in reversed(range(1, steps)):
+            act = lax.concatenate([act, swap_chip(act, k)], k)
+        blank = lax.slice(flat(x_all), (0, 0), (1, 1)) * 0
+        grad_w_in = jnp.broadcast_to(blank, w_in.shape)
+        act_all, grad_w_in = gather(act, grad_w_in)
         lead = act_all.shape[:-1]
 
         mixed = jnp.dot(flat(act_all), w_out, preferred_element_type=f32).astype(bf16).reshape(lead + (width,))
@@ -168,20 +167,20 @@
         other = [swap_core(own[0])]
         last = after(grad[..., quarter:], near_got)
         last_got = swap_chip(last, 0)
-        grad_w_in = weight_grad(own[0], x_rows[0], own_half, 0, jnp.zeros_like(w_in))
+        grad_w_in = weight_grad(own[0], x_rows[0], own_half, 0, grad_w_in)
         grad_w_in = weight_grad(other[0], x_rows[1], other_half, 0, grad_w_in)
         for bit in range(1, col_bits):
             kept, got = halve(mixed, bit)
             if bit + 1 < col_bits:
                 mixed = merged(kept, got)
-        own.append(lax.concatenate([last, after(last_got, grad_w_in)], 0))
+        last_got, got, grad_w_in = lax.optimization_barrier((last_got, got, grad_w_in))
+        own.append(lax.concatenate([last, last_got], 0))
         other.append(swap_core(own[1]))
         grad_w_in = weight_grad(own[1], x_rows[0], own_half, 1, grad_w_in)
         if col_bits > 1:
-            got = after(got, grad_w_in)
             mixed = merged(kept, got)
         mixed = flips(mixed, first, 0).reshape(tokens, width)
-        grad_w_in = weight_grad(after(other[1], got), x_rows[1], other_half, 1, grad_w_in)
+        grad_w_in = weight_grad(after(other[1], mixed), x_rows[1], other_half, 1, grad_w_in)
         return (mixed, grad_w_in, grad_w_out)
 
     return per_device

time: 195 us -> 186 us (0.954)
  waiting for transfers between devices: 93.1 us -> 82.6 us
  matrix products: 38.1 us -> 40.7 us
  starting transfers between devices: 31.1 us -> 28.5 us
  local copies, waits for them, and re-layouts: 12.8 us -> 14.8 us
    ppermute x14, waiting for transfers between devices: 53.4 us -> 48.5 us  [swap_chip(): lax.ppermute(v, 'row', [(i, i ^ 1 << orders[i & 1][step]) for i in range(...]
    ppermute x6, waiting for transfers between devices: 36.8 us -> 32.6 us  [swap_col(): return lax.ppermute(v, 'col', [(i, i ^ 1 << bit) for i in range(n_col)])]
    ppermute x14, starting transfers between devices: 19.3 us -> 16.5 us  [swap_chip(): lax.ppermute(v, 'row', [(i, i ^ 1 << orders[i & 1][step]) for i in range(...]
    dot_general x1, matrix products: 5.12 us -> 7.66 us  [per_device(): jnp.dot(flat(act_all), w_out, preferred_element_type=f32).astype(bf16)]
    unnamed x20 -> x22, local copies, waits for them, and re-layouts: 5.55 us -> 6.94 us
  transfers between devices with their start and end apart: 28 -> 28, of which waited for: 14 -> 15; matrix products, arithmetic and copies ran while one was open for 30% -> 30% of each run, Pallas kernels for 0% -> 0%
where the time goes in v3:
time: 186 us
  waiting for transfers between devices  82.6 us (44%)
  matrix products  40.7 us (22%)
  starting transfers between devices  28.5 us (15%)
  other arithmetic  17.3 us (9%)
  local copies, waits for them, and re-layouts  14.8 us (8%)
  between operations  1.91 us (1%)
    ppermute x14, waiting for transfers between devices, swap_chip(): lax.ppermute(v, 'row', [(i, i ^ 1 << orders[i & 1][step]) for i in range(...  48.5 us
    ppermute x6, waiting for transfers between devices, swap_col(): return lax.ppermute(v, 'col', [(i, i ^ 1 << bit) for i in range(n_col)])  32.6 us
    ppermute x14, starting transfers between devices, swap_chip(): lax.ppermute(v, 'row', [(i, i ^ 1 << orders[i & 1][step]) for i in range(...  16.5 us
    dot_general x4, matrix products, weight_grad(): out = jnp.dot(rows, flat(piece), preferred_element_type=f32).astype(bf16)  11.3 us
    ppermute x6, starting transfers between devices, swap_col(): return lax.ppermute(v, 'col', [(i, i ^ 1 << bit) for i in range(n_col)])  9.23 us
    dot_general x4, matrix products, up(): jnp.dot(flat(x), w_in[:, h], preferred_element_type=f32)  8.11 us
    dot_general x1, matrix products, per_device(): jnp.dot(flat(act_all), w_out, preferred_element_type=f32).astype(bf16)  7.66 us
    dot_general x1, matrix products, per_device(): lax.dot_general(flat(act_all), flat(c_all), (((0,), (0,)), ((), ())), pre...  7.64 us
  transfers between devices with their start and end apart: 28, of which 15 were waited for; matrix products, arithmetic and copies ran while one was open for 30% of the time, Pallas kernels for 0%

profile of v3, /device:TPU:0, one launch (start us, length us, event | category | flops | bytes accessed | tf_op | source)
XLA Modules:
  0.0 185.8 jit_solution(14290652134983673631)
XLA Ops:
  1.8 3.1 %collective-permute-start = (bf16[2,2,1,32,768]{4,3,2,1,0:T(8,128)(2,1)S(1)}, bf16[2,2,1,32,768]{4,3,2,1,0:T(8,128)(2,1)S(1)}, u32[]{:S(2)}, u32[]{:S(2)}) collective-permute-start(bf16[2,2,1,32,768]{4,3,2,1,0:T(8,128)(2,1)S(1)} %reverse_select_fusion.4), channel_id=1, source_target_pairs={{0,1},{1,0},{2,3},{3,2},{4,5},{5,4},{6,7},{7,6},{8,9},{9,8},{10,11... | collective-permute-start | bytes 589832 | tf_op jit(solution)/shard_map/ppermute | solution.py:30
  6.0 4.5 %collective-permute-done = bf16[2,2,1,32,768]{4,3,2,1,0:T(8,128)(2,1)S(1)} collective-permute-done((bf16[2,2,1,32,768]{4,3,2,1,0:T(8,128)(2,1)S(1)}, bf16[2,2,1,32,768]{4,3,2,1,0:T(8,128)(2,1)S(1)}, u32[]{:S(2)}, u32[]{:S(2)}) %collective-permute-start) | collective-permute-done | bytes 196640 | tf_op jit(solution)/shard_map/ppermute | solution.py:30
  10.6 3.9 %fusion.22 = bf16[256,3072]{1,0:T(8,128)(2,1)S(1)} fusion(bf16[256,768]{1,0:T(8,128)(2,1)S(1)} %bitcast.118, bf16[768,6144]{1,0:T(8,128)(2,1)} %param.5), kind=kOutput, calls=%fused_computation.20 | convolution fusion | flops 1208745984 | bytes 6684672 | tf_op jit(solution)/shard_map/dot_general | solution.py:81
  22.5 3.1 %collective-permute-start.4 = (bf16[2,2,2,32,768]{4,3,2,1,0:T(8,128)(2,1)S(1)}, bf16[2,2,2,32,768]{4,3,2,1,0:T(8,128)(2,1)S(1)}, u32[]{:S(2)}, u32[]{:S(2)}) collective-permute-start(bf16[2,2,2,32,768]{4,3,2,1,0:T(8,128)(2,1)S(1)} %pad_maximum_fusion.9), channel_id=1, source_target_pairs={{0,2},{1,3},{2,0},{3,1},{4,6},{5,7},{6,4},{7,5},{8,10},{9,11},{10,... | collective-permute-start | bytes 1179656 | tf_op jit(solution)/shard_map/ppermute | solution.py:30
  28.8 14.9 %collective-permute-done.4 = bf16[2,2,2,32,768]{4,3,2,1,0:T(8,128)(2,1)S(1)} collective-permute-done((bf16[2,2,2,32,768]{4,3,2,1,0:T(8,128)(2,1)S(1)}, bf16[2,2,2,32,768]{4,3,2,1,0:T(8,128)(2,1)S(1)}, u32[]{:S(2)}, u32[]{:S(2)}) %collective-permute-start.4) | collective-permute-done | bytes 393248 | tf_op jit(solution)/shard_map/ppermute | solution.py:30
  52.7 8.2 %collective-permute-done.3 = bf16[1,1,2,32,3072]{4,3,2,0,1:T(8,128)(2,1)S(1)} collective-permute-done((bf16[1,1,2,32,3072]{4,3,2,0,1:T(8,128)(2,1)S(1)}, bf16[1,1,2,32,3072]{4,3,2,0,1:T(8,128)(2,1)S(1)}, u32[]{:S(2)}, u32[]{:S(2)}) %collective-permute-start.3) | collective-permute-done | bytes 393248 | tf_op jit(solution)/shard_map/ppermute | solution.py:27
  60.9 2.2 %collective-permute-done.15 = bf16[1,2,2,32,3072]{4,3,2,0,1:T(8,128)(2,1)S(1)} collective-permute-done((bf16[1,2,2,32,3072]{4,3,2,0,1:T(8,128)(2,1)S(1)}, bf16[1,2,2,32,3072]{4,3,2,0,1:T(8,128)(2,1)S(1)}, u32[]{:S(2)}, u32[]{:S(2)}) %collective-permute-start.15) | collective-permute-done | bytes 786464 | tf_op jit(solution)/shard_map/ppermute | solution.py:27
  63.1 9.8 %collective-permute-done.17 = bf16[2,2,2,32,768]{4,3,2,1,0:T(8,128)(2,1)S(1)} collective-permute-done((bf16[2,2,2,32,768]{4,3,2,1,0:T(8,128)(2,1)S(1)}, bf16[2,2,2,32,768]{4,3,2,1,0:T(8,128)(2,1)S(1)}, u32[]{:S(2)}, u32[]{:S(2)}) %collective-permute-start.17) | collective-permute-done | bytes 393248 | tf_op jit(solution)/shard_map/ppermute | solution.py:30
  77.7 6.4 %collective-permute-done.9 = bf16[1,1,2,32,3072]{4,3,2,0,1:T(8,128)(2,1)S(1)} collective-permute-done((bf16[1,1,2,32,3072]{4,3,2,0,1:T(8,128)(2,1)S(1)}, bf16[1,1,2,32,3072]{4,3,2,0,1:T(8,128)(2,1)S(1)}, u32[]{:S(2)}, u32[]{:S(2)}) %collective-permute-start.9) | collective-permute-done | bytes 393248 | tf_op jit(solution)/shard_map/ppermute | solution.py:27
  86.9 9.7 %collective-permute-done.10 = bf16[1,1,4,32,3072]{4,3,2,0,1:T(8,128)(2,1)S(1)} collective-permute-done((bf16[1,1,4,32,3072]{4,3,2,0,1:T(8,128)(2,1)S(1)}, bf16[1,1,4,32,3072]{4,3,2,0,1:T(8,128)(2,1)S(1)}, u32[]{:S(2)}, u32[]{:S(2)}) %collective-permute-start.10) | collective-permute-done | bytes 786464 | tf_op jit(solution)/shard_map/ppermute | solution.py:27
  101.1 3.0 %collective-permute-done.16 = bf16[1,1,2,32,3072]{4,3,2,0,1:T(8,128)(2,1)S(1)} collective-permute-done((bf16[1,1,2,32,3072]{4,3,2,0,1:T(8,128)(2,1)S(1)}, bf16[1,1,2,32,3072]{4,3,2,0,1:T(8,128)(2,1)S(1)}, u32[]{:S(2)}, u32[]{:S(2)}) %collective-permute-start.16) | collective-permute-done | bytes 393248 | tf_op jit(solution)/shard_map/ppermute | solution.py:27
  105.5 3.3 %collective-permute-done.13 = bf16[1,2,4,32,1536]{4,3,2,0,1:T(8,128)(2,1)S(1)} collective-permute-done((bf16[1,2,4,32,1536]{4,3,2,0,1:T(8,128)(2,1)S(1)}, bf16[1,2,4,32,1536]{4,3,2,0,1:T(8,128)(2,1)S(1)}, u32[]{:S(2)}, u32[]{:S(2)}) %collective-permute-start.13) | collective-permute-done | bytes 786464 | tf_op jit(solution)/shard_map/ppermute | solution.py:27
  108.8 4.9 %broadcast_in_dim.8 = bf16[768,6144]{1,0:T(8,128)(2,1)} broadcast(bf16[]{:T(256)} %bitcast.18), dimensions={} | broadcast | bytes 9437186 | tf_op jit(solution)/shard_map/broadcast_in_dim | solution.py:128
  113.7 3.5 %collective-permute-done.19 = bf16[1,2,2,32,3072]{4,3,2,0,1:T(8,128)(2,1)S(1)} collective-permute-done((bf16[1,2,2,32,3072]{4,3,2,0,1:T(8,128)(2,1)S(1)}, bf16[1,2,2,32,3072]{4,3,2,0,1:T(8,128)(2,1)S(1)}, u32[]{:S(2)}, u32[]{:S(2)}) %collective-permute-start.19) | collective-permute-done | bytes 786464 | tf_op jit(solution)/shard_map/ppermute | solution.py:27
  119.5 10.4 %collective-permute-done.11 = bf16[1,2,4,32,1536]{4,3,2,0,1:T(8,128)(2,1)S(1)} collective-permute-done((bf16[1,2,4,32,1536]{4,3,2,0,1:T(8,128)(2,1)S(1)}, bf16[1,2,4,32,1536]{4,3,2,0,1:T(8,128)(2,1)S(1)}, u32[]{:S(2)}, u32[]{:S(2)}) %collective-permute-start.11) | collective-permute-done | bytes 786464 | tf_op jit(solution)/shard_map/ppermute | solution.py:27
  133.7 5.7 %pad_maximum_fusion = bf16[2,2,4,32,6144]{4,3,2,1,0:T(8,128)(2,1)S(1)} fusion(bf16[2,2,4,32,1536]{4,3,2,1,0:T(8,128)(2,1)S(1)} %get-tuple-element.36, bf16[2,2,4,32,1536]{4,3,2,1,0:T(8,128)(2,1)S(1)} %get-tuple-element.34, bf16[2,2,4,32,1536]{4,3,2,0,1:T(8,128)(2,1)S(1)} %get-tuple-element.33, bf16[2,2,4,32,1536]{4,3,2,0,1:T(8,128)(2,1)S(1)} %get-tuple-element.35), kind=kLoop, calls=%fused_computation.1 | loop fusion | flops 25165824 | bytes 12582912 | tf_op jit(solution)/shard_map/concatenate | solution.py:123
  139.4 7.7 %convolution_convert_fusion.4 = bf16[512,768]{1,0:T(8,128)(2,1)S(1)} fusion(bf16[512,6144]{1,0:T(8,128)(2,1)S(1)} %bitcast.87, bf16[6144,768]{1,0:T(8,128)(2,1)} %param.6), kind=kOutput, calls=%fused_computation.67 | convolution fusion | flops 4832231424 | bytes 16515072 | tf_op jit(solution)/shard_map/dot_general | solution.py:132
  149.8 7.6 %bitcast_convert_fusion = bf16[6144,768]{1,0:T(8,128)(2,1)} fusion(bf16[2,2,4,32,6144]{4,3,2,1,0:T(8,128)(2,1)S(1)} %pad_maximum_fusion, bf16[2,2,2,32,768]{4,3,2,1,0:T(8,128)(2,1)S(1)} %collective-permute-done.17, bf16[2,2,2,32,768]{4,3,2,1,0:T(8,128)(2,1)S(1)} %pad_maximum_fusion.10), kind=kOutput, calls=%fused_computation | convolution fusion | flops 4836950016 | bytes 16515072 | tf_op jit(solution)/shard_map/dot_general | solution.py:161
  164.7 2.8 %collective-permute-start.25 = (bf16[2,2,1,32,768]{4,3,2,1,0:T(8,128)(2,1)S(1)}, bf16[2,2,1,32,768]{4,3,2,1,0:T(8,128)(2,1)S(1)}, u32[]{:S(2)}, u32[]{:S(2)}) collective-permute-start(bf16[2,2,1,32,768]{4,3,2,1,0:T(8,128)(2,1)S(1)} %slice_bitcast_fusion), channel_id=1, source_target_pairs={{0,2},{1,3},{2,0},{3,1},{4,6},{5,7},{6,4},{7,5},{8,10},{9,11},{10,... | collective-permute-start | bytes 589832 | tf_op jit(solution)/shard_map/ppermute | solution.py:30
  167.5 2.8 %fusion.43 = bf16[768,6144]{1,0:T(8,128)(2,1)} fusion(bf16[768,6144]{1,0:T(8,128)(2,1)} %broadcast_in_dim.8, s32[]{:T(128)S(6)} %select_n.134, bf16[768,512]{0,1:T(8,128)(2,1)S(1)} %bitcast.112, bf16[512,1536]{1,0:T(8,128)(2,1)S(1)} %bitcast.106), kind=kOutput, calls=%fused_computation.33 | convolution fusion | flops 1209139200 | bytes 4718596 | tf_op jit(solution)/shard_map/dot_general | solution.py:152
  171.9 2.8 %fusion.42 = bf16[768,6144]{1,0:T(8,128)(2,1)} fusion(bf16[768,6144]{1,0:T(8,128)(2,1)} %fusion.43, s32[]{:T(128)S(6)} %select_n.137, bf16[768,512]{0,1:T(8,128)(2,1)S(1)} %bitcast.110, bf16[512,1536]{1,0:T(8,128)(2,1)S(1)} %bitcast.108), kind=kOutput, calls=%fused_computation.31 | convolution fusion | flops 1209139200 | bytes 4718596 | tf_op jit(solution)/shard_map/dot_general | solution.py:152
  174.7 2.3 %collective-permute-done.25 = bf16[2,2,1,32,768]{4,3,2,1,0:T(8,128)(2,1)S(1)} collective-permute-done((bf16[2,2,1,32,768]{4,3,2,1,0:T(8,128)(2,1)S(1)}, bf16[2,2,1,32,768]{4,3,2,1,0:T(8,128)(2,1)S(1)}, u32[]{:S(2)}, u32[]{:S(2)}) %collective-permute-start.25) | collective-permute-done | bytes 196640 | tf_op jit(solution)/shard_map/ppermute | solution.py:30
  179.0 2.8 %fusion.41 = bf16[768,6144]{1,0:T(8,128)(2,1)} fusion(bf16[768,6144]{1,0:T(8,128)(2,1)} %fusion.42, s32[]{:T(128)S(6)} %select_n.140, bf16[768,512]{0,1:T(8,128)(2,1)S(1)} %bitcast.113, bf16[512,1536]{1,0:T(8,128)(2,1)S(1)} %bitcast.105), kind=kOutput, calls=%fused_computation.29 | convolution fusion | flops 1209139200 | bytes 4718596 | tf_op jit(solution)/shard_map/dot_general | solution.py:152
  183.0 2.8 %fusion.40 = bf16[768,6144]{1,0:T(8,128)(2,1)} fusion(bf16[768,6144]{1,0:T(8,128)(2,1)} %fusion.41, s32[]{:T(128)S(6)} %select_n.141, bf16[768,512]{0,1:T(8,128)(2,1)S(1)} %bitcast.111, bf16[512,1536]{1,0:T(8,128)(2,1)S(1)} %bitcast.107), kind=kOutput, calls=%fused_computation.27 | convolution fusion | flops 1209139200 | bytes 4718596 | tf_op jit(solution)/shard_map/dot_general | solution.py:152
  (125 shorter events, 55.5 us)
Async XLA Ops:
  1.8 8.8 %collective-permute-start = (bf16[2,2,1,32,768]{4,3,2,1,0:T(8,128)(2,1)S(1)}, bf16[2,2,1,32,768]{4,3,2,1,0:T(8,128)(2,1)S(1)}, u32[]{:S(2)}, u32[]{:S(2)}) collective-permute-start(bf16[2,2,1,32,768]{4,3,2,1,0:T(8,128)(2,1)S(1)} %reverse_select_fusion.4), channel_id=1, source_target_pairs={{0,1},{1,0},{2,3},{3,2},{4,5},{5,4},{6,7},{7,6},{8,9},{9,8},{10,11... | collective-permute-start | bytes 589832 | tf_op jit(solution)/shard_map/ppermute | solution.py:30
  6.0 11.4 %collective-permute-start.5 = (bf16[2,2,1,32,768]{4,3,2,1,0:T(8,128)(2,1)S(1)}, bf16[2,2,1,32,768]{4,3,2,1,0:T(8,128)(2,1)S(1)}, u32[]{:S(2)}, u32[]{:S(2)}) collective-permute-start(bf16[2,2,1,32,768]{4,3,2,1,0:T(8,128)(2,1)S(1)} %reverse_select_fusion.2), channel_id=1, source_target_pairs={{0,1},{1,0},{2,3},{3,2},{4,5},{5,4},{6,7},{7,6},{8,9},{9,8},{10,11... | collective-permute-start | bytes 589832 | tf_op jit(solution)/shard_map/ppermute | solution.py:30
  17.2 8.4 %collective-permute-start.1 = (bf16[2,2,2,32,3072]{4,3,2,0,1:T(8,128)(2,1)S(1)}, bf16[2,2,2,32,3072]{4,3,2,0,1:T(8,128)(2,1)S(1)}, u32[]{:S(2)}, u32[]{:S(2)}) collective-permute-start(bf16[2,2,2,32,3072]{4,3,2,0,1:T(8,128)(2,1)S(1)} %broadcast_select_fusion.3), channel_id=1, source_target_pairs={{0,4},{4,0},{8,12},{12,8},{16,20},{20,16},{24,28},{28,24},{1,5},{5... | collective-permute-start | bytes 4718600 | tf_op jit(solution)/shard_map/ppermute | solution.py:24
  22.5 21.3 %collective-permute-start.4 = (bf16[2,2,2,32,768]{4,3,2,1,0:T(8,128)(2,1)S(1)}, bf16[2,2,2,32,768]{4,3,2,1,0:T(8,128)(2,1)S(1)}, u32[]{:S(2)}, u32[]{:S(2)}) collective-permute-start(bf16[2,2,2,32,768]{4,3,2,1,0:T(8,128)(2,1)S(1)} %pad_maximum_fusion.9), channel_id=1, source_target_pairs={{0,2},{1,3},{2,0},{3,1},{4,6},{5,7},{6,4},{7,5},{8,10},{9,11},{10,... | collective-permute-start | bytes 1179656 | tf_op jit(solution)/shard_map/ppermute | solution.py:30
  26.5 17.3 %collective-permute-start.2 = (bf16[1,2,2,32,3072]{4,3,2,0,1:T(8,128)(2,1)S(1)}, bf16[1,2,2,32,3072]{4,3,2,0,1:T(8,128)(2,1)S(1)}, u32[]{:S(2)}, u32[]{:S(2)}) collective-permute-start(bf16[1,2,2,32,3072]{4,3,2,0,1:T(8,128)(2,1)S(1)} %slice.122), channel_id=1, source_target_pairs={{0,8},{4,20},{8,0},{12,28},{16,24},{20,4},{24,16},{28,12},{1,9},{5... | collective-permute-start | bytes 2359304 | tf_op jit(solution)/shard_map/ppermute | solution.py:27
  46.9 16.3 %collective-permute-start.15 = (bf16[1,2,2,32,3072]{4,3,2,0,1:T(8,128)(2,1)S(1)}, bf16[1,2,2,32,3072]{4,3,2,0,1:T(8,128)(2,1)S(1)}, u32[]{:S(2)}, u32[]{:S(2)}) collective-permute-start(bf16[1,2,2,32,3072]{4,3,2,0,1:T(8,128)(2,1)S(1)} %slice.134), channel_id=1, source_target_pairs={{0,8},{4,20},{8,0},{12,28},{16,24},{20,4},{24,16},{28,12},{1,9},{5... | collective-permute-start | bytes 2359304 | tf_op jit(solution)/shard_map/ppermute | solution.py:27
  48.7 12.1 %collective-permute-start.3 = (bf16[1,1,2,32,3072]{4,3,2,0,1:T(8,128)(2,1)S(1)}, bf16[1,1,2,32,3072]{4,3,2,0,1:T(8,128)(2,1)S(1)}, u32[]{:S(2)}, u32[]{:S(2)}) collective-permute-start(bf16[1,1,2,32,3072]{4,3,2,0,1:T(8,128)(2,1)S(1)} %slice.124), channel_id=1, source_target_pairs={{0,16},{4,12},{8,24},{12,4},{16,0},{20,28},{24,8},{28,20},{1,17},{... | collective-permute-start | bytes 1179656 | tf_op jit(solution)/shard_map/ppermute | solution.py:27
  51.2 21.7 %collective-permute-start.8 = (bf16[1,2,2,32,3072]{4,3,2,0,1:T(8,128)(2,1)S(1)}, bf16[1,2,2,32,3072]{4,3,2,0,1:T(8,128)(2,1)S(1)}, u32[]{:S(2)}, u32[]{:S(2)}) collective-permute-start(bf16[1,2,2,32,3072]{4,3,2,0,1:T(8,128)(2,1)S(1)} %slice.126), channel_id=1, source_target_pairs={{0,8},{4,20},{8,0},{12,28},{16,24},{20,4},{24,16},{28,12},{1,9},{5... | collective-permute-start | bytes 2359304 | tf_op jit(solution)/shard_map/ppermute | solution.py:27
  52.7 20.2 %collective-permute-start.17 = (bf16[2,2,2,32,768]{4,3,2,1,0:T(8,128)(2,1)S(1)}, bf16[2,2,2,32,768]{4,3,2,1,0:T(8,128)(2,1)S(1)}, u32[]{:S(2)}, u32[]{:S(2)}) collective-permute-start(bf16[2,2,2,32,768]{4,3,2,1,0:T(8,128)(2,1)S(1)} %pad_maximum_fusion.10), channel_id=1, source_target_pairs={{0,2},{1,3},{2,0},{3,1},{4,6},{5,7},{6,4},{7,5},{8,10},{9,11},{10,... | collective-permute-start | bytes 1179656 | tf_op jit(solution)/shard_map/ppermute | solution.py:30
  76.2 7.8 %collective-permute-start.9 = (bf16[1,1,2,32,3072]{4,3,2,0,1:T(8,128)(2,1)S(1)}, bf16[1,1,2,32,3072]{4,3,2,0,1:T(8,128)(2,1)S(1)}, u32[]{:S(2)}, u32[]{:S(2)}) collective-permute-start(bf16[1,1,2,32,3072]{4,3,2,0,1:T(8,128)(2,1)S(1)} %slice.128), channel_id=1, source_target_pairs={{0,16},{4,12},{8,24},{12,4},{16,0},{20,28},{24,8},{28,20},{1,17},{... | collective-permute-start | bytes 1179656 | tf_op jit(solution)/shard_map/ppermute | solution.py:27
  76.9 21.4 %collective-permute-start.18 = (bf16[2,2,2,32,3072]{4,3,2,0,1:T(8,128)(2,1)S(1)}, bf16[2,2,2,32,3072]{4,3,2,0,1:T(8,128)(2,1)S(1)}, u32[]{:S(2)}, u32[]{:S(2)}) collective-permute-start(bf16[2,2,2,32,3072]{4,3,2,0,1:T(8,128)(2,1)S(1)} %broadcast_select_fusion), channel_id=1, source_target_pairs={{0,4},{4,0},{8,12},{12,8},{16,20},{20,16},{24,28},{28,24},{1,5},{5... | collective-permute-start | bytes 4718600 | tf_op jit(solution)/shard_map/ppermute | solution.py:24
  84.5 12.1 %collective-permute-start.10 = (bf16[1,1,4,32,3072]{4,3,2,0,1:T(8,128)(2,1)S(1)}, bf16[1,1,4,32,3072]{4,3,2,0,1:T(8,128)(2,1)S(1)}, u32[]{:S(2)}, u32[]{:S(2)}) collective-permute-start(bf16[1,1,4,32,3072]{4,3,2,0,1:T(8,128)(2,1)S(1)} %get-tuple-element.41), channel_id=1, source_target_pairs={{0,16},{4,12},{8,24},{12,4},{16,0},{20,28},{24,8},{28,20},{1,17},{... | collective-permute-start | bytes 2359304 | tf_op jit(solution)/shard_map/ppermute | solution.py:27
  85.3 18.8 %collective-permute-start.16 = (bf16[1,1,2,32,3072]{4,3,2,0,1:T(8,128)(2,1)S(1)}, bf16[1,1,2,32,3072]{4,3,2,0,1:T(8,128)(2,1)S(1)}, u32[]{:S(2)}, u32[]{:S(2)}) collective-permute-start(bf16[1,1,2,32,3072]{4,3,2,0,1:T(8,128)(2,1)S(1)} %slice.136), channel_id=1, source_target_pairs={{0,16},{4,12},{8,24},{12,4},{16,0},{20,28},{24,8},{28,20},{1,17},{... | collective-permute-start | bytes 1179656 | tf_op jit(solution)/shard_map/ppermute | solution.py:27
  96.8 12.1 %collective-permute-start.13 = (bf16[1,2,4,32,1536]{4,3,2,0,1:T(8,128)(2,1)S(1)}, bf16[1,2,4,32,1536]{4,3,2,0,1:T(8,128)(2,1)S(1)}, u32[]{:S(2)}, u32[]{:S(2)}) collective-permute-start(bf16[1,2,4,32,1536]{4,3,2,0,1:T(8,128)(2,1)S(1)} %get-tuple-element.40), channel_id=1, source_target_pairs={{0,8},{4,20},{8,0},{12,28},{16,24},{20,4},{24,16},{28,12},{1,9},{5... | collective-permute-start | bytes 2359304 | tf_op jit(solution)/shard_map/ppermute | solution.py:27
  99.2 18.0 %collective-permute-start.19 = (bf16[1,2,2,32,3072]{4,3,2,0,1:T(8,128)(2,1)S(1)}, bf16[1,2,2,32,3072]{4,3,2,0,1:T(8,128)(2,1)S(1)}, u32[]{:S(2)}, u32[]{:S(2)}) collective-permute-start(bf16[1,2,2,32,3072]{4,3,2,0,1:T(8,128)(2,1)S(1)} %slice.138), channel_id=1, source_target_pairs={{0,8},{4,20},{8,0},{12,28},{16,24},{20,4},{24,16},{28,12},{1,9},{5... | collective-permute-start | bytes 2359304 | tf_op jit(solution)/shard_map/ppermute | solution.py:27
  104.2 25.7 %collective-permute-start.11 = (bf16[1,2,4,32,1536]{4,3,2,0,1:T(8,128)(2,1)S(1)}, bf16[1,2,4,32,1536]{4,3,2,0,1:T(8,128)(2,1)S(1)}, u32[]{:S(2)}, u32[]{:S(2)}) collective-permute-start(bf16[1,2,4,32,1536]{4,3,2,0,1:T(8,128)(2,1)S(1)} %get-tuple-element.39), channel_id=1, source_target_pairs={{0,8},{4,20},{8,0},{12,28},{16,24},{20,4},{24,16},{28,12},{1,9},{5... | collective-permute-start | bytes 2359304 | tf_op jit(solution)/shard_map/ppermute | solution.py:27
  117.5 12.9 %collective-permute-start.20 = (bf16[1,1,2,32,3072]{4,3,2,0,1:T(8,128)(2,1)S(1)}, bf16[1,1,2,32,3072]{4,3,2,0,1:T(8,128)(2,1)S(1)}, u32[]{:S(2)}, u32[]{:S(2)}) collective-permute-start(bf16[1,1,2,32,3072]{4,3,2,0,1:T(8,128)(2,1)S(1)} %slice.140), channel_id=1, source_target_pairs={{0,16},{4,12},{8,24},{12,4},{16,0},{20,28},{24,8},{28,20},{1,17},{... | collective-permute-start | bytes 1179656 | tf_op jit(solution)/shard_map/ppermute | solution.py:27
  118.1 13.6 %collective-permute-start.14 = (bf16[2,2,4,32,1536]{4,3,2,0,1:T(8,128)(2,1)S(1)}, bf16[2,2,4,32,1536]{4,3,2,0,1:T(8,128)(2,1)S(1)}, u32[]{:S(2)}, u32[]{:S(2)}) collective-permute-start(bf16[2,2,4,32,1536]{4,3,2,0,1:T(8,128)(2,1)S(1)} %pad_maximum_fusion.3), channel_id=1, source_target_pairs={{0,4},{4,0},{8,12},{12,8},{16,20},{20,16},{24,28},{28,24},{1,5},{5... | collective-permute-start | bytes 4718600 | tf_op jit(solution)/shard_map/ppermute | solution.py:24
  131.2 16.0 %collective-permute-start.21 = (bf16[1,1,4,32,3072]{4,3,2,0,1:T(8,128)(2,1)S(1)}, bf16[1,1,4,32,3072]{4,3,2,0,1:T(8,128)(2,1)S(1)}, u32[]{:S(2)}, u32[]{:S(2)}) collective-permute-start(bf16[1,1,4,32,3072]{4,3,2,0,1:T(8,128)(2,1)S(1)} %fusion.49), channel_id=1, source_target_pairs={{0,16},{4,12},{8,24},{12,4},{16,0},{20,28},{24,8},{28,20},{1,17},{... | collective-permute-start | bytes 2359304 | tf_op jit(solution)/shard_map/ppermute | solution.py:27
  147.2 11.3 %collective-permute-start.23 = (bf16[2,2,2,32,768]{4,3,1,0,2:T(8,128)(2,1)S(1)}, bf16[2,2,2,32,768]{4,3,1,0,2:T(8,128)(2,1)S(1)}, u32[]{:S(2)}, u32[]{:S(2)}) collective-permute-start(bf16[2,2,2,32,768]{4,3,1,0,2:T(8,128)(2,1)S(1)} %bitcast.120), channel_id=1, source_target_pairs={{0,1},{1,0},{2,3},{3,2},{4,5},{5,4},{6,7},{7,6},{8,9},{9,8},{10,11... | collective-permute-start | bytes 1179656 | tf_op jit(solution)/shard_map/ppermute | solution.py:30
  148.3 12.0 %collective-permute-start.22 = (bf16[1,2,4,32,1536]{4,3,2,0,1:T(8,128)(2,1)S(1)}, bf16[1,2,4,32,1536]{4,3,2,0,1:T(8,128)(2,1)S(1)}, u32[]{:S(2)}, u32[]{:S(2)}) collective-permute-start(bf16[1,2,4,32,1536]{4,3,2,0,1:T(8,128)(2,1)S(1)} %get-tuple-element.43), channel_id=1, source_target_pairs={{0,8},{4,20},{8,0},{12,28},{16,24},{20,4},{24,16},{28,12},{1,9},{5... | collective-permute-start | bytes 2359304 | tf_op jit(solution)/shard_map/ppermute | solution.py:27
  160.5 9.9 %collective-permute-start.26 = (bf16[2,2,4,32,1536]{4,3,2,0,1:T(8,128)(2,1)S(1)}, bf16[2,2,4,32,1536]{4,3,2,0,1:T(8,128)(2,1)}, u32[]{:S(2)}, u32[]{:S(2)}) collective-permute-start(bf16[2,2,4,32,1536]{4,3,2,0,1:T(8,128)(2,1)S(1)} %pad_maximum_fusion.5), channel_id=1, source_target_pairs={{0,4},{4,0},{8,12},{12,8},{16,20},{20,16},{24,28},{28,24},{1,5},{5... | collective-permute-start | bytes 4718600 | tf_op jit(solution)/shard_map/ppermute | solution.py:24
  160.9 16.2 %collective-permute-start.24 = (bf16[1,2,4,32,1536]{4,3,2,0,1:T(8,128)(2,1)}, bf16[1,2,4,32,1536]{4,3,2,0,1:T(8,128)(2,1)S(1)}, u32[]{:S(2)}, u32[]{:S(2)}) collective-permute-start(bf16[1,2,4,32,1536]{4,3,2,0,1:T(8,128)(2,1)} %get-tuple-element.26), channel_id=1, source_target_pairs={{0,8},{4,20},{8,0},{12,28},{16,24},{20,4},{24,16},{28,12},{1,9},{5... | collective-permute-start | bytes 2359304 | tf_op jit(solution)/shard_map/ppermute | solution.py:27
  164.7 12.4 %collective-permute-start.25 = (bf16[2,2,1,32,768]{4,3,2,1,0:T(8,128)(2,1)S(1)}, bf16[2,2,1,32,768]{4,3,2,1,0:T(8,128)(2,1)S(1)}, u32[]{:S(2)}, u32[]{:S(2)}) collective-permute-start(bf16[2,2,1,32,768]{4,3,2,1,0:T(8,128)(2,1)S(1)} %slice_bitcast_fusion), channel_id=1, source_target_pairs={{0,2},{1,3},{2,0},{3,1},{4,6},{5,7},{6,4},{7,5},{8,10},{9,11},{10,... | collective-permute-start | bytes 589832 | tf_op jit(solution)/shard_map/ppermute | solution.py:30
  (14 other events, 53.4 us)

commit v4 on v3

--- a/solution.py
+++ b/solution.py
@@ -168,7 +168,6 @@
         last = after(grad[..., quarter:], near_got)
         last_got = swap_chip(last, 0)
         grad_w_in = weight_grad(own[0], x_rows[0], own_half, 0, grad_w_in)
-        grad_w_in = weight_grad(other[0], x_rows[1], other_half, 0, grad_w_in)
         for bit in range(1, col_bits):
             kept, got = halve(mixed, bit)
             if bit + 1 < col_bits:
@@ -176,6 +175,7 @@
         last_got, got, grad_w_in = lax.optimization_barrier((last_got, got, grad_w_in))
         own.append(lax.concatenate([last, last_got], 0))
         other.append(swap_core(own[1]))
+        grad_w_in = weight_grad(other[0], x_rows[1], other_half, 0, grad_w_in)
         grad_w_in = weight_grad(own[1], x_rows[0], own_half, 1, grad_w_in)
         if col_bits > 1:
             mixed = merged(kept, got)

time: 186 us -> 193 us (1.038)
  other arithmetic: 17.3 us -> 20.8 us
  matrix products: 40.7 us -> 42.9 us
    ppermute x6, waiting for transfers between devices: 32.6 us -> 38.4 us  [swap_col(): return lax.ppermute(v, 'col', [(i, i ^ 1 << bit) for i in range(n_col)])]
    ppermute x14, waiting for transfers between devices: 48.5 us -> 43.7 us  [swap_chip(): lax.ppermute(v, 'row', [(i, i ^ 1 << orders[i & 1][step]) for i in range(...]
    dot_general x4, matrix products: 5.95 us -> 10.6 us  [back(): lax.dot_general(flat(c), w_out[h], (((1,), (1,)), ((), ())), preferred_el...]
    slice x8, local copies, waits for them, and re-layouts: 0.32 us -> 2.91 us  [part(): return lax.slice_in_dim(v, index, index + 1, axis=axis)]
    dot_general x1, matrix products: 7.66 us -> 5.11 us  [per_device(): jnp.dot(flat(act_all), w_out, preferred_element_type=f32).astype(bf16)]
    convert_element_type x4, other arithmetic: 0.74 us -> 3.01 us  [scatter(): v = v.astype(bf16)]
    unnamed x22 -> x32, local copies, waits for them, and re-layouts: 6.94 us -> 4.79 us
    ppermute x8, starting transfers between devices: 2.79 us -> 0.72 us  [swap_core(): return lax.ppermute(v, 'row', [(i, i ^ 1) for i in range(n_row)])]
where the time goes in v4:
time: 193 us
  waiting for transfers between devices  82.6 us (43%)
  matrix products  42.9 us (22%)
  starting transfers between devices  28 us (15%)
  other arithmetic  20.8 us (11%)
  local copies, waits for them, and re-layouts  16.7 us (9%)
    ppermute x14, waiting for transfers between devices, swap_chip(): lax.ppermute(v, 'row', [(i, i ^ 1 << orders[i & 1][step]) for i in range(...  43.7 us
    ppermute x6, waiting for transfers between devices, swap_col(): return lax.ppermute(v, 'col', [(i, i ^ 1 << bit) for i in range(n_col)])  38.4 us
    ppermute x14, starting transfers between devices, swap_chip(): lax.ppermute(v, 'row', [(i, i ^ 1 << orders[i & 1][step]) for i in range(...  17.9 us
    dot_general x4, matrix products, weight_grad(): out = jnp.dot(rows, flat(piece), preferred_element_type=f32).astype(bf16)  11.3 us
    dot_general x4, matrix products, back(): lax.dot_general(flat(c), w_out[h], (((1,), (1,)), ((), ())), preferred_el...  10.6 us
    ppermute x6, starting transfers between devices, swap_col(): return lax.ppermute(v, 'col', [(i, i ^ 1 << bit) for i in range(n_col)])  9.37 us
    dot_general x4, matrix products, up(): jnp.dot(flat(x), w_in[:, h], preferred_element_type=f32)  8.21 us
    dot_general x1, matrix products, per_device(): lax.dot_general(flat(act_all), flat(c_all), (((0,), (0,)), ((), ())), pre...  7.64 us
  transfers between devices with their start and end apart: 28, of which 15 were waited for; matrix products, arithmetic and copies ran while one was open for 30% of the time, Pallas kernels for 0%

profile of v4, /device:TPU:0, one launch (start us, length us, event | category | flops | bytes accessed | tf_op | source)
XLA Modules:
  0.0 192.8 jit_solution(17202105008480293268)
XLA Ops:
  1.8 3.1 %collective-permute-start = (bf16[2,2,1,32,768]{4,3,2,1,0:T(8,128)(2,1)S(1)}, bf16[2,2,1,32,768]{4,3,2,1,0:T(8,128)(2,1)S(1)}, u32[]{:S(2)}, u32[]{:S(2)}) collective-permute-start(bf16[2,2,1,32,768]{4,3,2,1,0:T(8,128)(2,1)S(1)} %reverse_select_fusion.4), channel_id=1, source_target_pairs={{0,1},{1,0},{2,3},{3,2},{4,5},{5,4},{6,7},{7,6},{8,9},{9,8},{10,11... | collective-permute-start | bytes 589832 | tf_op jit(solution)/shard_map/ppermute | solution.py:30
  6.0 4.5 %collective-permute-done = bf16[2,2,1,32,768]{4,3,2,1,0:T(8,128)(2,1)S(1)} collective-permute-done((bf16[2,2,1,32,768]{4,3,2,1,0:T(8,128)(2,1)S(1)}, bf16[2,2,1,32,768]{4,3,2,1,0:T(8,128)(2,1)S(1)}, u32[]{:S(2)}, u32[]{:S(2)}) %collective-permute-start) | collective-permute-done | bytes 196640 | tf_op jit(solution)/shard_map/ppermute | solution.py:30
  10.6 3.9 %fusion.22 = bf16[256,3072]{1,0:T(8,128)(2,1)S(1)} fusion(bf16[256,768]{1,0:T(8,128)(2,1)S(1)} %bitcast.118, bf16[768,6144]{1,0:T(8,128)(2,1)} %param.5), kind=kOutput, calls=%fused_computation.20 | convolution fusion | flops 1208745984 | bytes 6684672 | tf_op jit(solution)/shard_map/dot_general | solution.py:81
  22.6 3.1 %collective-permute-start.4 = (bf16[2,2,2,32,768]{4,3,2,1,0:T(8,128)(2,1)S(1)}, bf16[2,2,2,32,768]{4,3,2,1,0:T(8,128)(2,1)S(1)}, u32[]{:S(2)}, u32[]{:S(2)}) collective-permute-start(bf16[2,2,2,32,768]{4,3,2,1,0:T(8,128)(2,1)S(1)} %pad_maximum_fusion.9), channel_id=1, source_target_pairs={{0,2},{1,3},{2,0},{3,1},{4,6},{5,7},{6,4},{7,5},{8,10},{9,11},{10,... | collective-permute-start | bytes 1179656 | tf_op jit(solution)/shard_map/ppermute | solution.py:30
  29.0 14.9 %collective-permute-done.4 = bf16[2,2,2,32,768]{4,3,2,1,0:T(8,128)(2,1)S(1)} collective-permute-done((bf16[2,2,2,32,768]{4,3,2,1,0:T(8,128)(2,1)S(1)}, bf16[2,2,2,32,768]{4,3,2,1,0:T(8,128)(2,1)S(1)}, u32[]{:S(2)}, u32[]{:S(2)}) %collective-permute-start.4) | collective-permute-done | bytes 393248 | tf_op jit(solution)/shard_map/ppermute | solution.py:30
  54.5 8.6 %collective-permute-done.3 = bf16[1,1,2,32,3072]{4,3,2,0,1:T(8,128)(2,1)} collective-permute-done((bf16[1,1,2,32,3072]{4,3,2,0,1:T(8,128)(2,1)}, bf16[1,1,2,32,3072]{4,3,2,0,1:T(8,128)(2,1)}, u32[]{:S(2)}, u32[]{:S(2)}) %collective-permute-start.3) | collective-permute-done | bytes 393248 | tf_op jit(solution)/shard_map/ppermute | solution.py:27
  64.6 10.1 %collective-permute-done.17 = bf16[2,2,2,32,768]{4,3,2,1,0:T(8,128)(2,1)S(1)} collective-permute-done((bf16[2,2,2,32,768]{4,3,2,1,0:T(8,128)(2,1)}, bf16[2,2,2,32,768]{4,3,2,1,0:T(8,128)(2,1)S(1)}, u32[]{:S(2)}, u32[]{:S(2)}) %collective-permute-start.17) | collective-permute-done | bytes 393248 | tf_op jit(solution)/shard_map/ppermute | solution.py:30
  74.6 4.0 %fusion.37 = bf16[256,3072]{1,0:T(8,128)(2,1)S(1)} fusion(bf16[256,768]{1,0:T(8,128)(2,1)S(1)} %bitcast.126, bf16[6144,768]{1,0:T(8,128)(2,1)} %param.6), kind=kOutput, calls=%fused_computation.25 | convolution fusion | flops 1208745984 | bytes 6684672 | tf_op jit(solution)/shard_map/dot_general | solution.py:86
  78.6 3.8 %fusion.31 = bf16[256,3072]{1,0:T(8,128)(2,1)S(1)} fusion(bf16[256,768]{1,0:T(8,128)(2,1)S(1)} %bitcast.127, bf16[6144,768]{1,0:T(8,128)(2,1)} %param.6), kind=kOutput, calls=%fused_computation.23 | convolution fusion | flops 1208745984 | bytes 6684672 | tf_op jit(solution)/shard_map/dot_general | solution.py:86
  85.6 6.0 %collective-permute-done.9 = bf16[1,1,2,32,3072]{4,3,2,0,1:T(8,128)(2,1)S(1)} collective-permute-done((bf16[1,1,2,32,3072]{4,3,2,0,1:T(8,128)(2,1)S(1)}, bf16[1,1,2,32,3072]{4,3,2,0,1:T(8,128)(2,1)S(1)}, u32[]{:S(2)}, u32[]{:S(2)}) %collective-permute-start.9) | collective-permute-done | bytes 393248 | tf_op jit(solution)/shard_map/ppermute | solution.py:27
  95.8 8.3 %collective-permute-done.10 = bf16[1,1,4,32,3072]{4,3,2,0,1:T(8,128)(2,1)S(1)} collective-permute-done((bf16[1,1,4,32,3072]{4,3,2,0,1:T(8,128)(2,1)S(1)}, bf16[1,1,4,32,3072]{4,3,2,0,1:T(8,128)(2,1)S(1)}, u32[]{:S(2)}, u32[]{:S(2)}) %collective-permute-start.10) | collective-permute-done | bytes 786464 | tf_op jit(solution)/shard_map/ppermute | solution.py:27
  113.5 2.9 %collective-permute-done.13 = bf16[1,2,4,32,1536]{4,3,2,0,1:T(8,128)(2,1)S(1)} collective-permute-done((bf16[1,2,4,32,1536]{4,3,2,0,1:T(8,128)(2,1)S(1)}, bf16[1,2,4,32,1536]{4,3,2,0,1:T(8,128)(2,1)S(1)}, u32[]{:S(2)}, u32[]{:S(2)}) %collective-permute-start.13) | collective-permute-done | bytes 786464 | tf_op jit(solution)/shard_map/ppermute | solution.py:27
  116.4 4.9 %broadcast_in_dim.8 = bf16[768,6144]{1,0:T(8,128)(2,1)} broadcast(bf16[]{:T(256)} %bitcast.18), dimensions={} | broadcast | bytes 9437186 | tf_op jit(solution)/shard_map/broadcast_in_dim | solution.py:128
  121.3 3.5 %collective-permute-done.19 = bf16[1,2,2,32,3072]{4,3,2,0,1:T(8,128)(2,1)S(1)} collective-permute-done((bf16[1,2,2,32,3072]{4,3,2,0,1:T(8,128)(2,1)S(1)}, bf16[1,2,2,32,3072]{4,3,2,0,1:T(8,128)(2,1)S(1)}, u32[]{:S(2)}, u32[]{:S(2)}) %collective-permute-start.19) | collective-permute-done | bytes 786464 | tf_op jit(solution)/shard_map/ppermute | solution.py:27
  126.8 10.6 %collective-permute-done.11 = bf16[1,2,4,32,1536]{4,3,2,0,1:T(8,128)(2,1)S(1)} collective-permute-done((bf16[1,2,4,32,1536]{4,3,2,0,1:T(8,128)(2,1)S(1)}, bf16[1,2,4,32,1536]{4,3,2,0,1:T(8,128)(2,1)S(1)}, u32[]{:S(2)}, u32[]{:S(2)}) %collective-permute-start.11) | collective-permute-done | bytes 786464 | tf_op jit(solution)/shard_map/ppermute | solution.py:27
  141.3 5.7 %pad_maximum_fusion = bf16[2,2,4,32,6144]{4,3,2,1,0:T(8,128)(2,1)S(1)} fusion(bf16[2,2,4,32,1536]{4,3,2,1,0:T(8,128)(2,1)S(1)} %get-tuple-element.36, bf16[2,2,4,32,1536]{4,3,2,1,0:T(8,128)(2,1)S(1)} %get-tuple-element.34, bf16[2,2,4,32,1536]{4,3,2,0,1:T(8,128)(2,1)S(1)} %get-tuple-element.33, bf16[2,2,4,32,1536]{4,3,2,0,1:T(8,128)(2,1)S(1)} %get-tuple-element.35), kind=kLoop, calls=%fused_computation.1 | loop fusion | flops 25165824 | bytes 12582912 | tf_op jit(solution)/shard_map/concatenate | solution.py:123
  147.0 5.1 %convolution_convert_fusion.4 = bf16[512,768]{1,0:T(8,128)(2,1)S(1)} fusion(bf16[512,6144]{1,0:T(8,128)(2,1)S(1)} %bitcast.87, bf16[6144,768]{1,0:T(8,128)(2,1)S(1)} %bitcast.125), kind=kOutput, calls=%fused_computation.67 | convolution fusion | flops 4832231424 | bytes 16515072 | tf_op jit(solution)/shard_map/dot_general | solution.py:132
  153.7 7.6 %bitcast_convert_fusion = bf16[6144,768]{1,0:T(8,128)(2,1)} fusion(bf16[2,2,4,32,6144]{4,3,2,1,0:T(8,128)(2,1)S(1)} %pad_maximum_fusion, bf16[2,2,2,32,768]{4,3,2,1,0:T(8,128)(2,1)S(1)} %collective-permute-done.17, bf16[2,2,2,32,768]{4,3,2,1,0:T(8,128)(2,1)S(1)} %copy-done.7), kind=kOutput, calls=%fused_computation | convolution fusion | flops 4836950016 | bytes 16515072 | tf_op jit(solution)/shard_map/dot_general | solution.py:161
  166.2 3.0 %collective-permute-start.25 = (bf16[2,2,1,32,768]{4,3,2,1,0:T(8,128)(2,1)S(1)}, bf16[2,2,1,32,768]{4,3,2,1,0:T(8,128)(2,1)S(1)}, u32[]{:S(2)}, u32[]{:S(2)}) collective-permute-start(bf16[2,2,1,32,768]{4,3,2,1,0:T(8,128)(2,1)S(1)} %slice_bitcast_fusion), channel_id=1, source_target_pairs={{0,2},{1,3},{2,0},{3,1},{4,6},{5,7},{6,4},{7,5},{8,10},{9,11},{10,... | collective-permute-start | bytes 589832 | tf_op jit(solution)/shard_map/ppermute | solution.py:30
  169.2 2.8 %fusion.43 = bf16[768,6144]{1,0:T(8,128)(2,1)} fusion(bf16[768,6144]{1,0:T(8,128)(2,1)} %broadcast_in_dim.8, s32[]{:T(128)S(6)} %select_n.134, bf16[768,512]{0,1:T(8,128)(2,1)S(1)} %bitcast.112, bf16[512,1536]{1,0:T(8,128)(2,1)S(1)} %bitcast.106), kind=kOutput, calls=%fused_computation.33 | convolution fusion | flops 1209139200 | bytes 4718596 | tf_op jit(solution)/shard_map/dot_general | solution.py:152
  172.1 6.7 %collective-permute-done.25 = bf16[2,2,1,32,768]{4,3,2,1,0:T(8,128)(2,1)S(1)} collective-permute-done((bf16[2,2,1,32,768]{4,3,2,1,0:T(8,128)(2,1)S(1)}, bf16[2,2,1,32,768]{4,3,2,1,0:T(8,128)(2,1)S(1)}, u32[]{:S(2)}, u32[]{:S(2)}) %collective-permute-start.25) | collective-permute-done | bytes 196640 | tf_op jit(solution)/shard_map/ppermute | solution.py:30
  182.8 2.8 %fusion.42 = bf16[768,6144]{1,0:T(8,128)(2,1)} fusion(bf16[768,6144]{1,0:T(8,128)(2,1)} %fusion.43, s32[]{:T(128)S(6)} %select_n.139, bf16[768,512]{0,1:T(8,128)(2,1)S(1)} %bitcast.110, bf16[512,1536]{1,0:T(8,128)(2,1)S(1)} %bitcast.108), kind=kOutput, calls=%fused_computation.31 | convolution fusion | flops 1209139200 | bytes 4718596 | tf_op jit(solution)/shard_map/dot_general | solution.py:152
  185.6 2.8 %fusion.41 = bf16[768,6144]{1,0:T(8,128)(2,1)} fusion(bf16[768,6144]{1,0:T(8,128)(2,1)} %fusion.42, s32[]{:T(128)S(6)} %select_n.140, bf16[768,512]{0,1:T(8,128)(2,1)S(1)} %bitcast.113, bf16[512,1536]{1,0:T(8,128)(2,1)S(1)} %bitcast.105), kind=kOutput, calls=%fused_computation.29 | convolution fusion | flops 1209139200 | bytes 4718596 | tf_op jit(solution)/shard_map/dot_general | solution.py:152
  190.0 2.8 %fusion.40 = bf16[768,6144]{1,0:T(8,128)(2,1)} fusion(bf16[768,6144]{1,0:T(8,128)(2,1)} %fusion.41, s32[]{:T(128)S(6)} %select_n.141, bf16[768,512]{0,1:T(8,128)(2,1)S(1)} %bitcast.111, bf16[512,1536]{1,0:T(8,128)(2,1)S(1)} %bitcast.107), kind=kOutput, calls=%fused_computation.27 | convolution fusion | flops 1209139200 | bytes 4718596 | tf_op jit(solution)/shard_map/dot_general | solution.py:152
  (136 shorter events, 59.3 us)
Async XLA Ops:
  1.8 8.8 %collective-permute-start = (bf16[2,2,1,32,768]{4,3,2,1,0:T(8,128)(2,1)S(1)}, bf16[2,2,1,32,768]{4,3,2,1,0:T(8,128)(2,1)S(1)}, u32[]{:S(2)}, u32[]{:S(2)}) collective-permute-start(bf16[2,2,1,32,768]{4,3,2,1,0:T(8,128)(2,1)S(1)} %reverse_select_fusion.4), channel_id=1, source_target_pairs={{0,1},{1,0},{2,3},{3,2},{4,5},{5,4},{6,7},{7,6},{8,9},{9,8},{10,11... | collective-permute-start | bytes 589832 | tf_op jit(solution)/shard_map/ppermute | solution.py:30
  6.0 11.4 %collective-permute-start.5 = (bf16[2,2,1,32,768]{4,3,2,1,0:T(8,128)(2,1)S(1)}, bf16[2,2,1,32,768]{4,3,2,1,0:T(8,128)(2,1)S(1)}, u32[]{:S(2)}, u32[]{:S(2)}) collective-permute-start(bf16[2,2,1,32,768]{4,3,2,1,0:T(8,128)(2,1)S(1)} %reverse_select_fusion.2), channel_id=1, source_target_pairs={{0,1},{1,0},{2,3},{3,2},{4,5},{5,4},{6,7},{7,6},{8,9},{9,8},{10,11... | collective-permute-start | bytes 589832 | tf_op jit(solution)/shard_map/ppermute | solution.py:30
  17.2 8.5 %collective-permute-start.1 = (bf16[2,2,2,32,3072]{4,3,2,0,1:T(8,128)(2,1)S(1)}, bf16[2,2,2,32,3072]{4,3,2,0,1:T(8,128)(2,1)S(1)}, u32[]{:S(2)}, u32[]{:S(2)}) collective-permute-start(bf16[2,2,2,32,3072]{4,3,2,0,1:T(8,128)(2,1)S(1)} %broadcast_select_fusion.3), channel_id=1, source_target_pairs={{0,4},{4,0},{8,12},{12,8},{16,20},{20,16},{24,28},{28,24},{1,5},{5... | collective-permute-start | bytes 4718600 | tf_op jit(solution)/shard_map/ppermute | solution.py:24
  22.6 21.3 %collective-permute-start.4 = (bf16[2,2,2,32,768]{4,3,2,1,0:T(8,128)(2,1)S(1)}, bf16[2,2,2,32,768]{4,3,2,1,0:T(8,128)(2,1)S(1)}, u32[]{:S(2)}, u32[]{:S(2)}) collective-permute-start(bf16[2,2,2,32,768]{4,3,2,1,0:T(8,128)(2,1)S(1)} %pad_maximum_fusion.9), channel_id=1, source_target_pairs={{0,2},{1,3},{2,0},{3,1},{4,6},{5,7},{6,4},{7,5},{8,10},{9,11},{10,... | collective-permute-start | bytes 1179656 | tf_op jit(solution)/shard_map/ppermute | solution.py:30
  26.6 17.3 %collective-permute-start.2 = (bf16[1,2,2,32,3072]{4,3,2,0,1:T(8,128)(2,1)S(1)}, bf16[1,2,2,32,3072]{4,3,2,0,1:T(8,128)(2,1)S(1)}, u32[]{:S(2)}, u32[]{:S(2)}) collective-permute-start(bf16[1,2,2,32,3072]{4,3,2,0,1:T(8,128)(2,1)S(1)} %slice.122), channel_id=1, source_target_pairs={{0,8},{4,20},{8,0},{12,28},{16,24},{20,4},{24,16},{28,12},{1,9},{5... | collective-permute-start | bytes 2359304 | tf_op jit(solution)/shard_map/ppermute | solution.py:27
  48.1 16.5 %collective-permute-start.15 = (bf16[1,2,2,32,3072]{4,3,2,0,1:T(8,128)(2,1)}, bf16[1,2,2,32,3072]{4,3,2,0,1:T(8,128)(2,1)}, u32[]{:S(2)}, u32[]{:S(2)}) collective-permute-start(bf16[1,2,2,32,3072]{4,3,2,0,1:T(8,128)(2,1)} %slice.134), channel_id=1, source_target_pairs={{0,8},{4,20},{8,0},{12,28},{16,24},{20,4},{24,16},{28,12},{1,9},{5... | collective-permute-start | bytes 2359304 | tf_op jit(solution)/shard_map/ppermute | solution.py:27
  50.7 12.4 %collective-permute-start.3 = (bf16[1,1,2,32,3072]{4,3,2,0,1:T(8,128)(2,1)}, bf16[1,1,2,32,3072]{4,3,2,0,1:T(8,128)(2,1)}, u32[]{:S(2)}, u32[]{:S(2)}) collective-permute-start(bf16[1,1,2,32,3072]{4,3,2,0,1:T(8,128)(2,1)} %slice.124), channel_id=1, source_target_pairs={{0,16},{4,12},{8,24},{12,4},{16,0},{20,28},{24,8},{28,20},{1,17},{... | collective-permute-start | bytes 1179656 | tf_op jit(solution)/shard_map/ppermute | solution.py:27
  53.9 20.7 %collective-permute-start.8 = (bf16[1,2,2,32,3072]{4,3,2,0,1:T(8,128)(2,1)}, bf16[1,2,2,32,3072]{4,3,2,0,1:T(8,128)(2,1)}, u32[]{:S(2)}, u32[]{:S(2)}) collective-permute-start(bf16[1,2,2,32,3072]{4,3,2,0,1:T(8,128)(2,1)} %slice.126), channel_id=1, source_target_pairs={{0,8},{4,20},{8,0},{12,28},{16,24},{20,4},{24,16},{28,12},{1,9},{5... | collective-permute-start | bytes 2359304 | tf_op jit(solution)/shard_map/ppermute | solution.py:27
  54.5 20.2 %collective-permute-start.17 = (bf16[2,2,2,32,768]{4,3,2,1,0:T(8,128)(2,1)}, bf16[2,2,2,32,768]{4,3,2,1,0:T(8,128)(2,1)S(1)}, u32[]{:S(2)}, u32[]{:S(2)}) collective-permute-start(bf16[2,2,2,32,768]{4,3,2,1,0:T(8,128)(2,1)} %copy-done.6), channel_id=1, source_target_pairs={{0,2},{1,3},{2,0},{3,1},{4,6},{5,7},{6,4},{7,5},{8,10},{9,11},{10,... | collective-permute-start | bytes 1179656 | tf_op jit(solution)/shard_map/ppermute | solution.py:30
  85.5 19.9 %collective-permute-start.18 = (bf16[2,2,2,32,3072]{4,3,2,0,1:T(8,128)(2,1)S(1)}, bf16[2,2,2,32,3072]{4,3,2,0,1:T(8,128)(2,1)S(1)}, u32[]{:S(2)}, u32[]{:S(2)}) collective-permute-start(bf16[2,2,2,32,3072]{4,3,2,0,1:T(8,128)(2,1)S(1)} %broadcast_select_fusion), channel_id=1, source_target_pairs={{0,4},{4,0},{8,12},{12,8},{16,20},{20,16},{24,28},{28,24},{1,5},{5... | collective-permute-start | bytes 4718600 | tf_op jit(solution)/shard_map/ppermute | solution.py:24
  92.1 12.1 %collective-permute-start.10 = (bf16[1,1,4,32,3072]{4,3,2,0,1:T(8,128)(2,1)S(1)}, bf16[1,1,4,32,3072]{4,3,2,0,1:T(8,128)(2,1)S(1)}, u32[]{:S(2)}, u32[]{:S(2)}) collective-permute-start(bf16[1,1,4,32,3072]{4,3,2,0,1:T(8,128)(2,1)S(1)} %get-tuple-element.41), channel_id=1, source_target_pairs={{0,16},{4,12},{8,24},{12,4},{16,0},{20,28},{24,8},{28,20},{1,17},{... | collective-permute-start | bytes 2359304 | tf_op jit(solution)/shard_map/ppermute | solution.py:27
  95.2 16.9 %collective-permute-start.16 = (bf16[1,1,2,32,3072]{4,3,2,0,1:T(8,128)(2,1)S(1)}, bf16[1,1,2,32,3072]{4,3,2,0,1:T(8,128)(2,1)S(1)}, u32[]{:S(2)}, u32[]{:S(2)}) collective-permute-start(bf16[1,1,2,32,3072]{4,3,2,0,1:T(8,128)(2,1)S(1)} %slice.136), channel_id=1, source_target_pairs={{0,16},{4,12},{8,24},{12,4},{16,0},{20,28},{24,8},{28,20},{1,17},{... | collective-permute-start | bytes 1179656 | tf_op jit(solution)/shard_map/ppermute | solution.py:27
  104.3 12.1 %collective-permute-start.13 = (bf16[1,2,4,32,1536]{4,3,2,0,1:T(8,128)(2,1)S(1)}, bf16[1,2,4,32,1536]{4,3,2,0,1:T(8,128)(2,1)S(1)}, u32[]{:S(2)}, u32[]{:S(2)}) collective-permute-start(bf16[1,2,4,32,1536]{4,3,2,0,1:T(8,128)(2,1)S(1)} %get-tuple-element.40), channel_id=1, source_target_pairs={{0,8},{4,20},{8,0},{12,28},{16,24},{20,4},{24,16},{28,12},{1,9},{5... | collective-permute-start | bytes 2359304 | tf_op jit(solution)/shard_map/ppermute | solution.py:27
  106.4 18.4 %collective-permute-start.19 = (bf16[1,2,2,32,3072]{4,3,2,0,1:T(8,128)(2,1)S(1)}, bf16[1,2,2,32,3072]{4,3,2,0,1:T(8,128)(2,1)S(1)}, u32[]{:S(2)}, u32[]{:S(2)}) collective-permute-start(bf16[1,2,2,32,3072]{4,3,2,0,1:T(8,128)(2,1)S(1)} %slice.138), channel_id=1, source_target_pairs={{0,8},{4,20},{8,0},{12,28},{16,24},{20,4},{24,16},{28,12},{1,9},{5... | collective-permute-start | bytes 2359304 | tf_op jit(solution)/shard_map/ppermute | solution.py:27
  112.2 25.3 %collective-permute-start.11 = (bf16[1,2,4,32,1536]{4,3,2,0,1:T(8,128)(2,1)S(1)}, bf16[1,2,4,32,1536]{4,3,2,0,1:T(8,128)(2,1)S(1)}, u32[]{:S(2)}, u32[]{:S(2)}) collective-permute-start(bf16[1,2,4,32,1536]{4,3,2,0,1:T(8,128)(2,1)S(1)} %get-tuple-element.39), channel_id=1, source_target_pairs={{0,8},{4,20},{8,0},{12,28},{16,24},{20,4},{24,16},{28,12},{1,9},{5... | collective-permute-start | bytes 2359304 | tf_op jit(solution)/shard_map/ppermute | solution.py:27
  125.0 12.9 %collective-permute-start.20 = (bf16[1,1,2,32,3072]{4,3,2,0,1:T(8,128)(2,1)S(1)}, bf16[1,1,2,32,3072]{4,3,2,0,1:T(8,128)(2,1)S(1)}, u32[]{:S(2)}, u32[]{:S(2)}) collective-permute-start(bf16[1,1,2,32,3072]{4,3,2,0,1:T(8,128)(2,1)S(1)} %slice.140), channel_id=1, source_target_pairs={{0,16},{4,12},{8,24},{12,4},{16,0},{20,28},{24,8},{28,20},{1,17},{... | collective-permute-start | bytes 1179656 | tf_op jit(solution)/shard_map/ppermute | solution.py:27
  126.8 13.6 %collective-permute-start.14 = (bf16[2,2,4,32,1536]{4,3,2,0,1:T(8,128)(2,1)S(1)}, bf16[2,2,4,32,1536]{4,3,2,0,1:T(8,128)(2,1)S(1)}, u32[]{:S(2)}, u32[]{:S(2)}) collective-permute-start(bf16[2,2,4,32,1536]{4,3,2,0,1:T(8,128)(2,1)S(1)} %pad_maximum_fusion.3), channel_id=1, source_target_pairs={{0,4},{4,0},{8,12},{12,8},{16,20},{20,16},{24,28},{28,24},{1,5},{5... | collective-permute-start | bytes 4718600 | tf_op jit(solution)/shard_map/ppermute | solution.py:24
  138.8 13.6 %collective-permute-start.21 = (bf16[1,1,4,32,3072]{4,3,2,0,1:T(8,128)(2,1)S(1)}, bf16[1,1,4,32,3072]{4,3,2,0,1:T(8,128)(2,1)S(1)}, u32[]{:S(2)}, u32[]{:S(2)}) collective-permute-start(bf16[1,1,4,32,3072]{4,3,2,0,1:T(8,128)(2,1)S(1)} %fusion.49), channel_id=1, source_target_pairs={{0,16},{4,12},{8,24},{12,4},{16,0},{20,28},{24,8},{28,20},{1,17},{... | collective-permute-start | bytes 2359304 | tf_op jit(solution)/shard_map/ppermute | solution.py:27
  152.3 11.3 %collective-permute-start.23 = (bf16[2,2,2,32,768]{4,3,1,0,2:T(8,128)(2,1)S(1)}, bf16[2,2,2,32,768]{4,3,1,0,2:T(8,128)(2,1)S(1)}, u32[]{:S(2)}, u32[]{:S(2)}) collective-permute-start(bf16[2,2,2,32,768]{4,3,1,0,2:T(8,128)(2,1)S(1)} %bitcast.120), channel_id=1, source_target_pairs={{0,1},{1,0},{2,3},{3,2},{4,5},{5,4},{6,7},{7,6},{8,9},{9,8},{10,11... | collective-permute-start | bytes 1179656 | tf_op jit(solution)/shard_map/ppermute | solution.py:30
  152.5 12.1 %collective-permute-start.22 = (bf16[1,2,4,32,1536]{4,3,2,0,1:T(8,128)(2,1)S(1)}, bf16[1,2,4,32,1536]{4,3,2,0,1:T(8,128)(2,1)S(1)}, u32[]{:S(2)}, u32[]{:S(2)}) collective-permute-start(bf16[1,2,4,32,1536]{4,3,2,0,1:T(8,128)(2,1)S(1)} %get-tuple-element.43), channel_id=1, source_target_pairs={{0,8},{4,20},{8,0},{12,28},{16,24},{20,4},{24,16},{28,12},{1,9},{5... | collective-permute-start | bytes 2359304 | tf_op jit(solution)/shard_map/ppermute | solution.py:27
  164.8 16.3 %collective-permute-start.26 = (bf16[2,2,4,32,1536]{4,3,2,0,1:T(8,128)(2,1)S(1)}, bf16[2,2,4,32,1536]{4,3,2,0,1:T(8,128)(2,1)}, u32[]{:S(2)}, u32[]{:S(2)}) collective-permute-start(bf16[2,2,4,32,1536]{4,3,2,0,1:T(8,128)(2,1)S(1)} %pad_maximum_fusion.5), channel_id=1, source_target_pairs={{0,4},{4,0},{8,12},{12,8},{16,20},{20,16},{24,28},{28,24},{1,5},{5... | collective-permute-start | bytes 4718600 | tf_op jit(solution)/shard_map/ppermute | solution.py:24
  164.9 13.8 %collective-permute-start.24 = (bf16[1,2,4,32,1536]{4,3,2,0,1:T(8,128)(2,1)S(1)}, bf16[1,2,4,32,1536]{4,3,2,0,1:T(8,128)(2,1)S(1)}, u32[]{:S(2)}, u32[]{:S(2)}) collective-permute-start(bf16[1,2,4,32,1536]{4,3,2,0,1:T(8,128)(2,1)S(1)} %get-tuple-element.26), channel_id=1, source_target_pairs={{0,8},{4,20},{8,0},{12,28},{16,24},{20,4},{24,16},{28,12},{1,9},{5... | collective-permute-start | bytes 2359304 | tf_op jit(solution)/shard_map/ppermute | solution.py:27
  166.2 12.6 %collective-permute-start.25 = (bf16[2,2,1,32,768]{4,3,2,1,0:T(8,128)(2,1)S(1)}, bf16[2,2,1,32,768]{4,3,2,1,0:T(8,128)(2,1)S(1)}, u32[]{:S(2)}, u32[]{:S(2)}) collective-permute-start(bf16[2,2,1,32,768]{4,3,2,1,0:T(8,128)(2,1)S(1)} %slice_bitcast_fusion), channel_id=1, source_target_pairs={{0,2},{1,3},{2,0},{3,1},{4,6},{5,7},{6,4},{7,5},{8,10},{9,11},{10,... | collective-permute-start | bytes 589832 | tf_op jit(solution)/shard_map/ppermute | solution.py:30
  179.4 9.0 %collective-permute-start.27 = (bf16[2,2,4,32,1536]{4,3,2,0,1:T(8,128)(2,1)S(1)}, bf16[2,2,4,32,1536]{4,3,2,0,1:T(8,128)(2,1)}, u32[]{:S(2)}, u32[]{:S(2)}) collective-permute-start(bf16[2,2,4,32,1536]{4,3,2,0,1:T(8,128)(2,1)S(1)} %constant_dynamic-update-slice_fusion), channel_id=1, source_target_pairs={{0,4},{4,0},{8,12},{12,8},{16,20},{20,16},{24,28},{28,24},{1,5},{5... | collective-permute-start | bytes 4718600 | tf_op jit(solution)/shard_map/ppermute | solution.py:24
  (19 other events, 127.4 us)
